TPU v7x, 128 devices: a whole 4x4x4 slice. The times are simulated.
128 devices in a mesh: tile: 64 (over z, x, y), slab: 2 (over core).
Axes of the slice: x: 4, y: 4, z: 4, core: 2. Of those that a mesh axis runs over, the one named last changes fastest.
Arguments:
- gas_state: float32 [4, 256, 16, 256], P(None, 'tile', None, 'slab'), may hold values from -6 to 6
- sound_speed: float32 [256, 16, 256], P('tile', None, 'slab'), may hold values from 0.5 to 2
- velocity: float32 [3, 64, 2, 32768], P(None, 'tile', 'slab'), may hold values from -6 to 6
- drag_rate: float32 [64, 2, 32768], P('tile', 'slab'), may hold values from 0.05 to 0.9
- parcel_mass: float32 [64, 2, 32768], P('tile', 'slab'), may hold values from 0.2 to 5
- cell_offset: float32 [64, 2, 32768], P('tile', 'slab'), may hold values from -0.5 to 0.5
- target_owner: int32 [64, 2, 32768, 1], P('tile', 'slab'), may hold values from 0 to 127; in each aligned block of 32768 rows (0 to 32767, 32768 to 65535, ..., all dimensions but the last counted through in order) at most 384 rows name the same one
- target_cell: int32 [64, 2, 32768], P('tile', 'slab'), may hold values from 0 to 8191
- live_counts: int32 [64, 2], P('tile', 'slab'), may hold values from 10922 to 32768
Outputs:
- gas_next: float32 [4, 256, 16, 256], P(None, 'tile', None, 'slab')
- moved_velocity: float32 [3, 64, 2, 128, 384], P(None, 'tile', 'slab')
Inputs may be any that keep to these rules, and one draw needn't show every extreme that they name: `target_owner`: in each owner's 32768 slots, live or not, at most 384 name the same new owner.
All inputs are finite; a program needn't handle non-finite values.
Results may differ from a plain program's by a relative error of at most 0.0003.
Values sent between devices are 32-bit elements; how exact they have to be, the bound alone decides.
No kernel may reach another device: no remote copies, remote signals or barrier semaphores. Data moves between devices by JAX's collectives and lax.ppermute only.
A program may use at most 192 MiB of HBM per device.

v0:
```python
import jax
import jax.numpy as jnp
from jax import lax
from jax.sharding import PartitionSpec as P

courant = 0.4


def passed_along(value, axis, steps):
    count = lax.axis_size(axis)
    pairs = [(source, (source + steps) % count) for source in range(count)]
    return lax.ppermute(value, axis, pairs)


def with_halo(block, sides, width, periodic):
    for axis, dim in sides:
        count = lax.axis_size(axis)
        forward = [(i, i + 1) for i in range(count - 1)]
        if periodic:
            forward.append((count - 1, 0))
        backward = [(target, source) for source, target in forward]
        low = lax.ppermute(
            lax.slice_in_dim(block, block.shape[dim] - width, None, axis=dim), axis, forward
        )
        high = lax.ppermute(lax.slice_in_dim(block, 0, width, axis=dim), axis, backward)
        block = jnp.concatenate([low, block, high], axis=dim)
    return block


def fourth(extended, dimension, length):

    def window(position):
        return lax.slice_in_dim(extended, position, position + length, axis=dimension)

    return (8.0 * (window(3) - window(1)) - (window(4) - window(0))) / 12.0


def periodic_extend(field, dimension):
    head = lax.slice_in_dim(
        field, field.shape[dimension] - 2, field.shape[dimension], axis=dimension
    )
    tail = lax.slice_in_dim(field, 0, 2, axis=dimension)
    return jnp.concatenate([head, field, tail], axis=dimension)


def per_device(
    gas_state,
    sound_speed,
    velocity,
    drag_rate,
    parcel_mass,
    cell_offset,
    target_owner,
    target_cell,
    live_counts,
):
    tile_count = lax.axis_size("tile")
    slab_count = lax.axis_size("slab")
    owner_count = tile_count * slab_count
    slot_count = target_cell.shape[-1]
    capacity = 3 * slot_count // (2 * owner_count)
    width_x = gas_state.shape[1]
    width_y = gas_state.shape[2]
    width_z = gas_state.shape[3]
    plane_size = width_y * width_z
    alive_mask = lax.iota(jnp.int32, slot_count) < live_counts.reshape(())
    destination = jnp.where(alive_mask, target_owner.reshape(slot_count), owner_count)
    ordering = jnp.argsort(destination, stable=True)
    tallies = jnp.zeros((owner_count + 1,), jnp.int32).at[destination].add(1)
    firsts = jnp.cumsum(tallies) - tallies
    sorted_owner = destination[ordering]
    placed = lax.iota(jnp.int32, slot_count) - firsts[sorted_owner]
    ranking = jnp.zeros((slot_count,), jnp.int32).at[ordering].set(placed)
    slot_index = destination * capacity + ranking
    payload = jnp.concatenate(
        [
            velocity.reshape(3, slot_count),
            drag_rate.reshape(1, slot_count),
            parcel_mass.reshape(1, slot_count),
            cell_offset.reshape(1, slot_count),
            target_cell.reshape(1, slot_count).astype(jnp.float32),
        ],
        axis=0,
    )
    outbox = (
        jnp.zeros((7, owner_count * capacity), jnp.float32)
        .at[:, slot_index]
        .set(payload, mode="drop")
    )
    arrived = lax.all_to_all(
        outbox.reshape(7, owner_count, capacity),
        ("tile", "slab"),
        split_axis=1,
        concat_axis=1,
        tiled=True,
    )
    arrived = arrived.reshape(7, owner_count * capacity)
    cell_ids = arrived[6].astype(jnp.int32)
    momentum_flat = gas_state[1:4].reshape(3, width_x * plane_size)
    gas_speed = jnp.take(momentum_flat, cell_ids, axis=1)
    speeds = arrived[0:3]
    rates = arrived[3]
    masses = arrived[4]
    shifts = arrived[5]
    occupied = masses > 0.0
    relaxed = jnp.where(occupied[None, :], speeds + rates[None, :] * (gas_speed - speeds), 0.0)
    moved_velocity = relaxed.reshape(3, 1, 1, owner_count, capacity)
    kicked = (masses * rates)[None, :] * (speeds - gas_speed)
    weight_low = 0.5 * (0.5 - shifts) ** 2
    weight_mid = 0.75 - shifts**2
    weight_high = 0.5 * (0.5 + shifts) ** 2
    center_index = cell_ids + plane_size
    deposit = jnp.zeros((3, (width_x + 2) * plane_size), jnp.float32)
    deposit = deposit.at[:, center_index - plane_size].add(kicked * weight_low[None, :])
    deposit = deposit.at[:, center_index].add(kicked * weight_mid[None, :])
    deposit = deposit.at[:, center_index + plane_size].add(kicked * weight_high[None, :])
    deposit = deposit.reshape(3, width_x + 2, width_y, width_z)
    left_rim = deposit[:, 0]
    right_rim = deposit[:, width_x + 1]
    momentum = gas_state[1:4] + deposit[:, 1 : width_x + 1]
    pressure = sound_speed * gas_state[0]
    from_right = passed_along(left_rim, "tile", -1)
    from_left = passed_along(right_rim, "tile", 1)
    momentum = momentum.at[:, 0].add(from_left).at[:, width_x - 1].add(from_right)
    edges = with_halo(jnp.stack([pressure, momentum[0]]), (("tile", 1),), 2, True)
    pressure_x = edges[0]
    first_x = edges[1]
    vertical = with_halo(jnp.stack([pressure, momentum[2]]), (("slab", 3),), 2, False)
    density_next = gas_state[0] - courant * (
        fourth(first_x, 0, width_x)
        + fourth(periodic_extend(momentum[1], 1), 1, width_y)
        + fourth(vertical[1], 2, width_z)
    )
    first_next = momentum[0] - courant * fourth(pressure_x, 0, width_x)
    second_next = momentum[1] - courant * fourth(periodic_extend(pressure, 1), 1, width_y)
    third_next = momentum[2] - courant * fourth(vertical[0], 2, width_z)
    gas_next = jnp.stack([density_next, first_next, second_next, third_next])
    return (gas_next, moved_velocity)


def solution(mesh):
    return jax.shard_map(
        per_device,
        mesh=mesh,
        in_specs=(
            P(None, "tile", None, "slab"),
            P("tile", None, "slab"),
            P(None, "tile", "slab", None),
            P("tile", "slab", None),
            P("tile", "slab", None),
            P("tile", "slab", None),
            P("tile", "slab", None, None),
            P("tile", "slab", None),
            P("tile", "slab"),
        ),
        out_specs=(P(None, "tile", None, "slab"), P(None, "tile", "slab", None, None)),
        check_vma=False,
    )
```

profile of v0, /device:TPU:0, one launch (start us, length us, event | category | flops | bytes accessed | tf_op | source)
XLA Modules:
  0.0 2177.4 jit_solution(12437869138338529148)
XLA Ops:
  3.4 226.3 %scatter_custom_fusion = s32[129]{0:T(256)S(1)} fusion(s32[32768]{0:T(1024)S(1)} %bitcast.123, s32[32768]{0:T(1024)S(1)} %broadcast.299, s32[]{:T(128)} %constant.105.clone.1), kind=kCustom, calls=%fused_computation.138 | custom fusion | flops 32768 | bytes 520 | tf_op jit(solution)/shard_map/scatter-add | solution.py:69
  231.3 11.2 sort.17
  242.5 181.0 %gather_fusion = s32[32768]{0:T(1024)S(1)} fusion(s32[32768]{0:T(1024)S(1)} %fusion.17, s32[32768]{0:T(1024)S(1)} %get-tuple-element.50), kind=kCustom, calls=%fused_computation | custom fusion | bytes 393216 | tf_op jit(solution)/shard_map/gather | solution.py:71
  423.8 202.2 %gather_fusion.1 = s32[32768]{0:T(1024)S(1)} fusion(s32[129]{0:T(256)S(1)} %slice_subtract_fusion.8, s32[32768]{0:T(1024)S(1)} %broadcast_clamp_fusion.1), kind=kCustom, calls=%fused_computation.1 | custom fusion | bytes 393216 | tf_op jit(solution)/shard_map/gather | solution.py:72
  627.4 9.0 copy.36
  636.4 120.1 %scatter_custom_fusion.1 = s32[32768]{0:T(1024)S(1)} fusion(s32[32768]{0:T(1024)S(1)} %get-tuple-element.51, s32[32768]{0:T(1024)S(1)} %iota_subtract_fusion, s32[]{:T(128)} %constant.105.clone.1), kind=kCustom, calls=%fused_computation.67 | custom fusion | bytes 131076 | tf_op jit(solution)/shard_map/scatter | solution.py:73
  756.6 90.3 %scatter_custom_fusion.2 = f32[7,49152]{0,1:T(8,128)} fusion(s32[32768]{0:T(1024)S(1)} %compare_select_fusion.9, f32[32768,7]{1,0:T(8,128)} %copy.36, f32[]{:T(128)} %constant.102.clone.1), kind=kCustom, calls=%fused_computation.24 | custom fusion | bytes 1376768 | tf_op jit(solution)/shard_map/scatter | solution.py:88
  847.0 14.4 copy.37
  861.4 11.3 all-to-all-start
  872.7 2.6 copy.41
  875.4 22.1 %all-to-all-done = f32[7,128,384]{2,0,1:T(8,128)S(1)} async-done(((f32[7,128,384]{2,0,1:T(8,128)}), f32[7,128,384]{2,0,1:T(8,128)S(1)}, u32[]{:S(2)}, u32[]{:S(2)}) %all-to-all-start) | async-done | bytes 1376288 | tf_op jit(solution)/shard_map/all_to_all | solution.py:90
  902.4 165.2 %gather_fusion.2 = f32[49152,3]{1,0:T(8,128)} fusion(f32[3,8192]{0,1:T(8,128)} %bitcast.98, s32[49152]{0:T(1024)S(1)} %broadcast_clamp_fusion), kind=kCustom, calls=%fused_computation.2 | custom fusion | bytes 1376256 | tf_op jit(solution)/shard_map/jit(_take)/gather | solution.py:100
  1067.6 13.9 copy.45
  1083.9 12.3 copy.40
  1096.3 25.2 %fusion.7 = f32[3,49152]{0,1:T(8,128)} fusion(f32[49152,3]{1,0:T(8,128)} %gather_fusion.2, f32[3,128,384]{0,2,1:T(8,128)} %copy.40, f32[49152]{0:T(1024)} %mul.122, pred[49152]{0:T(1024)(128)(4,1)S(1)} %compare_and_fusion.1), kind=kLoop, calls=%fused_computation.17 | loop fusion | flops 442368 | bytes 2015232 | tf_op jit(solution)/shard_map/mul | solution.py:108
  1121.5 319.1 %scatter_custom_fusion.3 = f32[3,12288]{0,1:T(8,128)} fusion(s32[49152]{0:T(1024)} %bitcast.119, f32[3,49152]{0,1:T(8,128)} %fusion.7, f32[49152]{0:T(1024)S(1)} %bitcast.113, f32[]{:T(128)} %constant.102.clone.1), kind=kCustom, calls=%fused_computation.13 | custom fusion | flops 294912 | bytes 25510400 | tf_op jit(solution)/shard_map/scatter-add | solution.py:114
  1440.5 306.5 %scatter_custom_fusion.4 = f32[3,12288]{0,1:T(8,128)} fusion(f32[3,12288]{0,1:T(8,128)} %scatter_custom_fusion.3, s32[49152]{0:T(1024)} %bitcast.118, f32[3,49152]{0,1:T(8,128)} %fusion.7, f32[49152]{0:T(1024)S(1)} %bitcast.112), kind=kCustom, calls=%fused_computation.11 | custom fusion | flops 294912 | bytes 25509888 | tf_op jit(solution)/shard_map/scatter-add | solution.py:115
  1747.0 306.7 %scatter_custom_fusion.5 = f32[3,12288]{0,1:T(8,128)} fusion(f32[3,12288]{0,1:T(8,128)} %scatter_custom_fusion.4, s32[49152]{0:T(1024)} %bitcast.117, f32[3,49152]{0,1:T(8,128)} %fusion.7, f32[49152]{0:T(1024)S(1)} %bitcast.111), kind=kCustom, calls=%fused_computation.9 | custom fusion | flops 294912 | bytes 25509888 | tf_op jit(solution)/shard_map/scatter-add | solution.py:116
  2055.4 4.6 slice.318
  2060.0 2.8 copy.51
  2063.2 89.3 %collective-permute-start = (f32[3,16,128]{2,1,0:T(8,128)S(1)}, f32[3,16,128]{2,1,0:T(8,128)S(1)}, u32[]{:S(2)}, u32[]{:S(2)}) collective-permute-start(f32[3,16,128]{2,1,0:T(8,128)S(1)} %bitcast.124), channel_id=1, source_target_pairs={{0,2},{2,4},{4,6},{6,8},{8,10},{10,12},{12,14},{14,16},{16,18},{18... | collective-permute-start | bytes 73736 | tf_op jit(solution)/shard_map/ppermute | solution.py:12
  2154.0 2.7 collective-permute-done.1
  2156.7 5.5 collective-permute-start.2
  2163.8 7.7 collective-permute-done.3
  (80 shorter events, 23.4 us)
Async XLA Ops:
  423.7 202.3 %copy-start.6 = (f32[3,1,1,32768]{3,2,1,0:T(1,128)S(1)}, f32[3,1,1,32768]{3,2,1,0:T(1,128)}, u32[]{:S(2)}) copy-start(f32[3,1,1,32768]{3,2,1,0:T(1,128)} %param.15) | copy-start | bytes 1179652
  423.7 202.6 %copy-start.7 = (f32[1,1,32768]{2,1,0:T(1,128)S(1)}, f32[1,1,32768]{2,1,0:T(1,128)}, u32[]{:S(2)}) copy-start(f32[1,1,32768]{2,1,0:T(1,128)} %param.16) | copy-start | bytes 393220
  423.7 202.6 %copy-start.8 = (f32[1,1,32768]{2,1,0:T(1,128)S(1)}, f32[1,1,32768]{2,1,0:T(1,128)}, u32[]{:S(2)}) copy-start(f32[1,1,32768]{2,1,0:T(1,128)} %param.17) | copy-start | bytes 393220
  423.7 202.6 %copy-start.9 = (f32[1,1,32768]{2,1,0:T(1,128)S(1)}, f32[1,1,32768]{2,1,0:T(1,128)}, u32[]{:S(2)}) copy-start(f32[1,1,32768]{2,1,0:T(1,128)} %param.18) | copy-start | bytes 393220
  423.7 332.8 %copy-start.1 = (s32[1,1,32768,1]{2,3,1,0:T(1,128)S(1)}, s32[1,1,32768,1]{2,3,1,0:T(1,128)}, u32[]{:S(2)}) copy-start(s32[1,1,32768,1]{2,3,1,0:T(1,128)} %param.19) | copy-start | bytes 393220
  756.6 116.1 %slice-start = ((f32[4,4,16,128]{3,2,1,0:T(8,128)}), f32[3,4,16,128]{3,2,1,0:T(8,128)S(1)}, s32[]{:S(2)}) async-start(f32[4,4,16,128]{3,2,1,0:T(8,128)} %param.13), calls=%async_computation.1 | async-start | bytes 196608 | tf_op jit(solution)/shard_map/slice | solution.py:120
  756.6 118.7 %copy-start.4 = (f32[4,4,16,128]{3,2,1,0:T(8,128)S(1)}, f32[4,4,16,128]{3,2,1,0:T(8,128)}, u32[]{:S(2)}) copy-start(f32[4,4,16,128]{3,2,1,0:T(8,128)} %param.13) | copy-start | bytes 393220
  756.6 118.7 %copy-start.10 = (f32[4,16,128]{2,1,0:T(8,128)S(1)}, f32[4,16,128]{2,1,0:T(8,128)}, u32[]{:S(2)}) copy-start(f32[4,16,128]{2,1,0:T(8,128)} %param.14) | copy-start | bytes 98308
  861.4 36.1 %all-to-all-start = ((f32[7,128,384]{2,0,1:T(8,128)}), f32[7,128,384]{2,0,1:T(8,128)S(1)}, u32[]{:S(2)}, u32[]{:S(2)}) async-start(f32[7,128,384]{2,0,1:T(8,128)} %copy.37), calls=%async_computation | async-start | bytes 3145728 | tf_op jit(solution)/shard_map/all_to_all | solution.py:90
  1096.3 25.2 %copy-start.3 = (f32[1,128,384]{2,0,1:T(1,128)S(1)}, f32[1,128,384]{2,0,1:T(1,128)}, u32[]{:S(2)}) copy-start(f32[1,128,384]{2,0,1:T(1,128)} %get-tuple-element.39) | copy-start | bytes 589828
  1121.4 319.1 %copy-start.2 = (f32[1,128,384]{2,0,1:T(1,128)S(1)}, f32[1,128,384]{2,0,1:T(1,128)}, u32[]{:S(2)}) copy-start(f32[1,128,384]{2,0,1:T(1,128)} %get-tuple-element.37) | copy-start | bytes 589828
  1747.0 405.5 %copy-start.5 = (f32[4,4,16,128]{3,2,1,0:T(8,128)S(1)}, f32[4,4,16,128]{3,2,1,0:T(8,128)}, u32[]{:S(2)}) copy-start(f32[4,4,16,128]{3,2,1,0:T(8,128)} %param.13) | copy-start | bytes 393220
  1747.0 415.3 %copy-start = (f32[3,1,1,128,384]{4,0,3,2,1:T(4,128)S(1)}, f32[3,1,1,128,384]{4,0,3,2,1:T(4,128)}, u32[]{:S(2)}) copy-start(f32[3,1,1,128,384]{4,0,3,2,1:T(4,128)} %get-tuple-element.34) | copy-start | bytes 1769476
  2063.2 90.8 %collective-permute-start = (f32[3,16,128]{2,1,0:T(8,128)S(1)}, f32[3,16,128]{2,1,0:T(8,128)S(1)}, u32[]{:S(2)}, u32[]{:S(2)}) collective-permute-start(f32[3,16,128]{2,1,0:T(8,128)S(1)} %bitcast.124), channel_id=1, source_target_pairs={{0,2},{2,4},{4,6},{6,8},{8,10},{10,12},{12,14},{14,16},{16,18},{18... | collective-permute-start | bytes 73736 | tf_op jit(solution)/shard_map/ppermute | solution.py:12
  2152.8 3.9 collective-permute-start.1
  2156.7 7.1 collective-permute-start.2
  2162.2 9.3 collective-permute-start.3
  2171.7 2.6 collective-permute-start.4
  2173.0 3.1 collective-permute-start.5
where the time goes:
time: 2200 us; the launch traced here: 2180 us
  other arithmetic  1210 us (55%)
  local copies, waits for them, and re-layouts  824 us (37%)
  starting transfers between devices  109 us (5%)
  waiting for transfers between devices  36.2 us (2%)
    scatter-add x1, other arithmetic, per_device(): deposit.at[:, center_index - plane_size].add(kicked * weight_low[None, :])  319 us
    scatter-add x1, other arithmetic, per_device(): deposit.at[:, center_index + plane_size].add(kicked * weight_high[None, :])  307 us
    scatter-add x1, other arithmetic, per_device(): deposit = deposit.at[:, center_index].add(kicked * weight_mid[None, :])  306 us
    scatter-add x1, other arithmetic, per_device(): tallies = jnp.zeros((owner_count + 1,), jnp.int32).at[destination].add(1)  226 us
    gather x1, local copies, waits for them, and re-layouts, per_device(): placed = lax.iota(jnp.int32, slot_count) - firsts[sorted_owner]  202 us
    gather x1, local copies, waits for them, and re-layouts, per_device(): sorted_owner = destination[ordering]  181 us
    gather x2, local copies, waits for them, and re-layouts, per_device(): gas_speed = jnp.take(momentum_flat, cell_ids, axis=1)  179 us
    scatter x1, local copies, waits for them, and re-layouts, per_device(): ranking = jnp.zeros((slot_count,), jnp.int32).at[ordering].set(placed)  120 us
  transfers between devices with their start and end apart: 7, of which 6 were waited for; matrix products, arithmetic and copies ran while one was open for 0% of the time, Pallas kernels for 0%

commit v1 on v0

v1 whole, which is shorter than its diff:
```python
import jax
import jax.numpy as jnp
from jax import lax
from jax.experimental import pallas as pl
from jax.experimental.pallas import tpu as pltpu
from jax.sharding import PartitionSpec as P

courant = 0.4
LANES = 128
COLUMNS = 256
RES = 64
ROWS = 16
SOURCES = 8
FIELDS = 7
VMEM_BYTES = 40 * 1024 * 1024
NT = (((1,), (1,)), ((), ()))
NN = (((1,), (0,)), ((), ()))


def split2(x):
    hi = x.astype(jnp.bfloat16).astype(jnp.float32)
    return hi, x - hi


def dispatch_kernel(
    live_ref, vel_ref, rate_ref, mass_ref, off_ref, owner_ref, cell_ref, out_ref,
    acc, values, lead, onehot, owners, base, combined,
):
    owner_count = base.shape[0]
    windows = acc.shape[1]
    groups = acc.shape[2]
    pitch = out_ref.shape[0] // owner_count
    chunk = ROWS * LANES
    step = pl.program_id(0)
    f32, bf16 = jnp.float32, jnp.bfloat16

    @pl.when(step == 0)
    def _():
        acc[...] = jnp.zeros_like(acc)
        base[...] = jnp.zeros_like(base)

    slot = (
        step * chunk
        + lax.broadcasted_iota(jnp.int32, (ROWS, LANES), 0) * LANES
        + lax.broadcasted_iota(jnp.int32, (ROWS, LANES), 1)
    )
    alive = slot < live_ref[0, 0]
    dest = jnp.where(alive, owner_ref[...], owner_count)

    owner_row = lax.broadcasted_iota(jnp.int32, (owner_count, LANES), 0)
    for j in range(ROWS):
        owners[:, j * LANES : (j + 1) * LANES] = jnp.where(
            dest[j : j + 1, :] == owner_row, 1.0, 0.0
        ).astype(bf16)
    before = lax.broadcasted_iota(jnp.int32, (COLUMNS, COLUMNS), 0)
    after = lax.broadcasted_iota(jnp.int32, (COLUMNS, COLUMNS), 1)
    upper = jnp.where(before < after, 1.0, 0.0).astype(bf16)
    ones = jnp.full((COLUMNS, LANES), 1.0, bf16)
    start = base[...]
    running = start * float(chunk)
    for t in range(ROWS // 2):
        tile = owners[:, t * COLUMNS : (t + 1) * COLUMNS]
        prior = lax.dot_general(tile, upper, NN, preferred_element_type=f32)
        count = lax.dot_general(tile, ones, NN, preferred_element_type=f32)
        for half in range(2):
            j = 2 * t + half
            total = prior[:, half * LANES : (half + 1) * LANES] + running
            mask = dest[j : j + 1, :] == owner_row
            combined[j : j + 1, :] = jnp.sum(
                jnp.where(mask, total, 0.0), axis=0, keepdims=True
            )
        running = running + count
    tally = running - start * float(chunk)
    base[...] = start + tally
    passes = (jnp.max(tally).astype(jnp.int32) + RES - 1) // RES
    both = combined[...].astype(jnp.int32)
    local_rank = both & (chunk - 1)
    rank = local_rank + both // chunk
    column = (dest // groups) * RES + (rank & (RES - 1))
    turn = jnp.where(alive, local_rank // RES, -1)
    group = dest & (groups - 1)

    fields = [
        vel_ref[0], vel_ref[1], vel_ref[2], rate_ref[...], mass_ref[...], off_ref[...],
        cell_ref[...].astype(f32),
    ]
    group_row = lax.broadcasted_iota(jnp.int32, (groups, LANES), 0)
    width = FIELDS * groups
    for v, field in enumerate(fields):
        hi, lo = split2(field)
        values[v] = hi
        values[v + FIELDS] = lo
    for j in range(ROWS):
        mask = group[j : j + 1, :] == group_row
        for v in range(2 * FIELDS):
            lead[v * groups : (v + 1) * groups, j * LANES : (j + 1) * LANES] = jnp.where(
                mask, values[v, j : j + 1, :], 0.0
            ).astype(bf16)

    column_row = lax.broadcasted_iota(jnp.int32, (COLUMNS, LANES), 0)
    lane = lax.broadcasted_iota(jnp.int32, (groups, LANES), 1)
    starts = start.astype(jnp.int32)

    def one_pass(number, carry):
        picked = jnp.where(turn == number, column, -1)
        for j in range(ROWS):
            onehot[:, j * LANES : (j + 1) * LANES] = jnp.where(
                picked[j : j + 1, :] == column_row, 1.0, 0.0
            ).astype(bf16)
        product = lax.dot_general(lead[...], onehot[...], NT, preferred_element_type=f32)
        product = product[:width] + product[width:]
        for k in range(COLUMNS // LANES):
            cols = slice(k * LANES, (k + 1) * LANES)
            even = starts[2 * k * groups : (2 * k + 1) * groups]
            odd = starts[(2 * k + 1) * groups : (2 * k + 2) * groups]
            first = jnp.where(lane < RES, even, odd) + number * RES
            window = (first + (((lane & (RES - 1)) - first) & (RES - 1))) // RES
            for w in range(windows):
                here = window == w
                for v in range(FIELDS):
                    acc[v, w, :, cols] += jnp.where(
                        here, product[v * groups : (v + 1) * groups, cols], 0.0
                    )
        return carry

    lax.fori_loop(0, passes, one_pass, 0)

    @pl.when(step == pl.num_programs(0) - 1)
    def _():
        low = lax.broadcasted_iota(jnp.int32, (8, LANES), 1) < RES
        for v in range(FIELDS):
            for k in range(COLUMNS // LANES):
                cols = slice(k * LANES, (k + 1) * LANES)
                for m in range(windows // 2):
                    for part in range(groups // 8):
                        rows = slice(part * 8, (part + 1) * 8)
                        one = acc[v, 2 * m, rows, cols]
                        two = acc[v, 2 * m + 1, rows, cols]
                        place = v * (windows // 2) + m
                        even = (2 * k * groups + part * 8) * pitch + place
                        odd = ((2 * k + 1) * groups + part * 8) * pitch + place
                        out_ref[pl.ds(even, 8, stride=pitch), :] = jnp.where(
                            low, one, pltpu.roll(two, RES, 1)
                        )
                        out_ref[pl.ds(odd, 8, stride=pitch), :] = jnp.where(
                            low, pltpu.roll(one, RES, 1), two
                        )


def dispatch(live, vel, rate, mass, off, owner, cell, owner_count, capacity):
    rows = rate.shape[0]
    groups = owner_count * RES // COLUMNS
    chunk = ROWS * LANES
    pitch = FIELDS * capacity // LANES
    plain = pl.BlockSpec((ROWS, LANES), lambda i: (i, 0))
    return pl.pallas_call(
        dispatch_kernel,
        grid=(rows // ROWS,),
        in_specs=[
            pl.BlockSpec(memory_space=pltpu.SMEM),
            pl.BlockSpec((3, ROWS, LANES), lambda i: (0, i, 0)),
            plain, plain, plain, plain, plain,
        ],
        out_specs=pl.BlockSpec((owner_count * pitch, LANES), lambda i: (0, 0)),
        out_shape=jax.ShapeDtypeStruct((owner_count * pitch, LANES), jnp.float32),
        scratch_shapes=[
            pltpu.VMEM((FIELDS, capacity // RES, groups, COLUMNS), jnp.float32),
            pltpu.VMEM((2 * FIELDS, ROWS, LANES), jnp.float32),
            pltpu.VMEM((2 * FIELDS * groups, chunk), jnp.bfloat16),
            pltpu.VMEM((COLUMNS, chunk), jnp.bfloat16),
            pltpu.VMEM((owner_count, chunk), jnp.bfloat16),
            pltpu.VMEM((owner_count, LANES), jnp.float32),
            pltpu.VMEM((ROWS, LANES), jnp.float32),
        ],
        compiler_params=pltpu.CompilerParams(vmem_limit_bytes=VMEM_BYTES),
        name="dispatch",
    )(live, vel, rate, mass, off, owner, cell)


def deposit_kernel(
    arrived_ref, gas_ref, moved_ref, dep_ref, table, total, onehot, lead, speeds, pieces
):
    capacity = moved_ref.shape[2]
    width_x = gas_ref.shape[1]
    reach = width_x + 2
    strips = 8
    rows = width_x * strips
    pitch = arrived_ref.shape[0] // SOURCES
    parts = capacity // LANES
    f32, bf16 = jnp.float32, jnp.bfloat16
    step = pl.program_id(0)

    @pl.when(step == 0)
    def _():
        total[...] = jnp.zeros_like(total)
        for v in range(3):
            for x in range(0, width_x, 2):
                for h in range(2):
                    two = [gas_ref[1 + v, x + i, h * 8 : (h + 1) * 8, :] for i in range(2)]
                    hi, lo = split2(jnp.concatenate(two, axis=0))
                    at = v * rows + x * strips
                    cols = slice(h * LANES, (h + 1) * LANES)
                    table[at : at + 16, cols] = hi.astype(bf16)
                    table[3 * rows + at : 3 * rows + at + 16, cols] = lo.astype(bf16)

    def field(v):
        return jnp.concatenate(
            [arrived_ref[pl.ds(v * parts + m, SOURCES, stride=pitch), :] for m in range(parts)],
            axis=1,
        )

    cell = field(6).astype(jnp.int32)
    column = (cell & (LANES - 1)) + ((cell >> 10) & 1) * LANES
    plane = cell >> 11
    strip = (cell >> 7) & 7
    row = plane * strips + strip
    column_row = lax.broadcasted_iota(jnp.int32, (COLUMNS, capacity), 0)
    for s in range(SOURCES):
        onehot[:, s * capacity : (s + 1) * capacity] = jnp.where(
            column[s : s + 1, :] == column_row, 1.0, 0.0
        ).astype(bf16)
    found = lax.dot_general(table[...], onehot[...], NN, preferred_element_type=f32)
    found = found[: 3 * rows] + found[3 * rows :]
    row_row = lax.broadcasted_iota(jnp.int32, (rows, capacity), 0)
    for s in range(SOURCES):
        mask = row[s : s + 1, :] == row_row
        for v in range(3):
            speeds[v, s : s + 1, :] = jnp.sum(
                jnp.where(
                    mask,
                    found[v * rows : (v + 1) * rows, s * capacity : (s + 1) * capacity],
                    0.0,
                ),
                axis=0,
                keepdims=True,
            )
    rate = field(3)
    mass = field(4)
    shift = field(5)
    occupied = mass > 0.0
    low_weight = 0.5 * (0.5 - shift) ** 2
    mid_weight = 0.75 - shift**2
    high_weight = 0.5 * (0.5 + shift) ** 2
    weights = []
    for x in range(reach):
        weights.append(
            jnp.where(
                plane == x,
                low_weight,
                jnp.where(plane == x - 1, mid_weight, jnp.where(plane == x - 2, high_weight, 0.0)),
            )
        )
    for v in range(3):
        speed = field(v)
        slip = speed - speeds[v]
        moved_ref[v] = jnp.where(occupied, speed - rate * slip, 0.0)
        kick = mass * rate * slip
        for x in range(reach):
            hi, lo = split2(kick * weights[x])
            pieces[v * reach + x] = hi
            pieces[(3 + v) * reach + x] = lo
    strip_row = lax.broadcasted_iota(jnp.int32, (strips, capacity), 0)
    for s in range(SOURCES):
        mask = strip[s : s + 1, :] == strip_row
        for pair in range(3 * reach):
            both = [jnp.where(mask, pieces[2 * pair + i, s : s + 1, :], 0.0) for i in range(2)]
            lead[pair * 16 : (pair + 1) * 16, s * capacity : (s + 1) * capacity] = (
                jnp.concatenate(both, axis=0).astype(bf16)
            )
    half = 3 * reach * strips
    product = lax.dot_general(lead[...], onehot[...], NT, preferred_element_type=f32)
    total[...] = total[...] + (product[:half] + product[half:])

    @pl.when(step == pl.num_programs(0) - 1)
    def _():
        for v in range(3):
            for x in range(reach):
                at = (v * reach + x) * strips
                for h in range(2):
                    dep_ref[v, x, h * 8 : (h + 1) * 8, :] = total[
                        at : at + strips, h * LANES : (h + 1) * LANES
                    ]


def deposit(arrived, gas, count, capacity):
    pitch = arrived.shape[0] // count
    width_x, width_y, width_z = gas.shape[1:]
    reach = width_x + 2
    deposit_rows = 3 * reach * 8
    return pl.pallas_call(
        deposit_kernel,
        grid=(count // SOURCES,),
        in_specs=[
            pl.BlockSpec((SOURCES * pitch, LANES), lambda i: (i, 0)),
            pl.BlockSpec(gas.shape, lambda i: (0, 0, 0, 0)),
        ],
        out_specs=[
            pl.BlockSpec((3, SOURCES, capacity), lambda i: (0, i, 0)),
            pl.BlockSpec((3, reach, width_y, width_z), lambda i: (0, 0, 0, 0)),
        ],
        out_shape=[
            jax.ShapeDtypeStruct((3, count, capacity), jnp.float32),
            jax.ShapeDtypeStruct((3, reach, width_y, width_z), jnp.float32),
        ],
        scratch_shapes=[
            pltpu.VMEM((6 * width_x * 8, COLUMNS), jnp.bfloat16),
            pltpu.VMEM((deposit_rows, COLUMNS), jnp.float32),
            pltpu.VMEM((COLUMNS, SOURCES * capacity), jnp.bfloat16),
            pltpu.VMEM((2 * deposit_rows, SOURCES * capacity), jnp.bfloat16),
            pltpu.VMEM((3, SOURCES, capacity), jnp.float32),
            pltpu.VMEM((6 * reach, SOURCES, capacity), jnp.float32),
        ],
        compiler_params=pltpu.CompilerParams(vmem_limit_bytes=VMEM_BYTES),
        name="deposit",
    )(arrived, gas)


def step_kernel(
    slab_ref, gas_ref, sound_ref, dep_ref, left_ref, right_ref, other_ref,
    left_other_ref, right_other_ref, left_p_ref, right_p_ref, other_p_ref, next_ref,
):
    width_x, width_y, width_z = sound_ref.shape
    slab = slab_ref[0, 0]
    first_slab = slab == 0
    lane = lax.broadcasted_iota(jnp.int32, (width_y, width_z), 1)

    def along_y(f, shift):
        return pltpu.roll(f, (-shift) % width_y, 0)

    def along_z(f, other, shift):
        turned = pltpu.roll(f, (-shift) % width_z, 1)
        beyond = pltpu.roll(other, (-shift) % width_z, 1)
        if shift > 0:
            inside = lane < width_z - shift
            reached = first_slab
        else:
            inside = lane >= -shift
            reached = jnp.logical_not(first_slab)
        return jnp.where(inside, turned, jnp.where(reached, beyond, 0.0))

    def fourth(shifted):
        return (8.0 * (shifted(1) - shifted(-1)) - (shifted(2) - shifted(-2))) / 12.0

    def momentum(k, x):
        value = gas_ref[1 + k, x] + dep_ref[k, x + 1]
        if x == 0:
            value = value + left_ref[2 + k]
        if x == width_x - 1:
            value = value + right_ref[2 + k]
        return value

    planes = [[momentum(k, x) for x in range(width_x)] for k in range(3)]
    first = {x: planes[0][x] for x in range(width_x)}
    first[-2] = left_ref[0]
    first[-1] = left_ref[1] + dep_ref[0, 0]
    first[width_x] = right_ref[0] + dep_ref[0, width_x + 1]
    first[width_x + 1] = right_ref[1]
    pressure = {x: sound_ref[x] * gas_ref[0, x] for x in range(width_x)}
    pressure[-2] = left_p_ref[0]
    pressure[-1] = left_p_ref[1]
    pressure[width_x] = right_p_ref[0]
    pressure[width_x + 1] = right_p_ref[1]
    for x in range(width_x):
        other = other_ref[x]
        if x == 0:
            other = other + left_other_ref[...]
        if x == width_x - 1:
            other = other + right_other_ref[...]
        other_p = other_p_ref[x]
        p = pressure[x]
        next_ref[0, x] = gas_ref[0, x] - courant * (
            fourth(lambda s: first[x + s])
            + fourth(lambda s: along_y(planes[1][x], s))
            + fourth(lambda s: along_z(planes[2][x], other, s))
        )
        next_ref[1, x] = planes[0][x] - courant * fourth(lambda s: pressure[x + s])
        next_ref[2, x] = planes[1][x] - courant * fourth(lambda s: along_y(p, s))
        next_ref[3, x] = planes[2][x] - courant * fourth(lambda s: along_z(p, other_p, s))


def gas_step(slab, gas, *rest):
    whole = pl.BlockSpec(memory_space=pltpu.VMEM)
    return pl.pallas_call(
        step_kernel,
        in_specs=[pl.BlockSpec(memory_space=pltpu.SMEM)] + [whole] * (1 + len(rest)),
        out_specs=whole,
        out_shape=jax.ShapeDtypeStruct(gas.shape, jnp.float32),
        compiler_params=pltpu.CompilerParams(vmem_limit_bytes=VMEM_BYTES),
        name="gas_step",
    )(slab, gas, *rest)


def per_device(
    gas_state, sound_speed, velocity, drag_rate, parcel_mass, cell_offset, target_owner,
    target_cell, live_counts,
):
    tiles = lax.axis_size("tile")
    slabs = lax.axis_size("slab")
    owner_count = tiles * slabs
    slot_count = target_cell.shape[-1]
    capacity = 3 * slot_count // (2 * owner_count)
    width_x = gas_state.shape[1]
    rows = slot_count // LANES
    to_right = [(t, (t + 1) % tiles) for t in range(tiles)]
    to_left = [(t, (t - 1) % tiles) for t in range(tiles)]
    swap = [(s, slabs - 1 - s) for s in range(slabs)]

    def diagonal(pairs):
        return [(a * slabs + s, b * slabs + r) for a, b in pairs for s, r in swap]

    pressure = sound_speed * gas_state[0]
    left_p = lax.ppermute(pressure[width_x - 2 :], "tile", to_right)
    right_p = lax.ppermute(pressure[:2], "tile", to_left)
    other_p = lax.ppermute(pressure, "slab", swap)

    outbox = dispatch(
        live_counts,
        velocity.reshape(3, rows, LANES),
        drag_rate.reshape(rows, LANES),
        parcel_mass.reshape(rows, LANES),
        cell_offset.reshape(rows, LANES),
        target_owner.reshape(rows, LANES),
        target_cell.reshape(rows, LANES),
        owner_count,
        capacity,
    )
    arrived = lax.all_to_all(
        outbox.reshape(owner_count, 1, FIELDS * capacity), ("tile", "slab"),
        split_axis=0, concat_axis=0, tiled=True,
    ).reshape(outbox.shape)
    moved, dep = deposit(arrived, gas_state, owner_count, capacity)

    first = gas_state[1] + dep[0, 1 : width_x + 1]
    left = lax.ppermute(
        jnp.concatenate([first[width_x - 2 :], dep[:, width_x + 1]]), "tile", to_right
    )
    right = lax.ppermute(jnp.concatenate([first[:2], dep[:, 0]]), "tile", to_left)
    other = lax.ppermute(gas_state[3] + dep[2, 1 : width_x + 1], "slab", swap)
    left_other = lax.ppermute(dep[2, width_x + 1], ("tile", "slab"), diagonal(to_right))
    right_other = lax.ppermute(dep[2, 0], ("tile", "slab"), diagonal(to_left))
    slab = lax.axis_index("slab").astype(jnp.int32).reshape(1, 1)
    gas_next = gas_step(
        slab, gas_state, sound_speed, dep, left, right, other, left_other, right_other,
        left_p, right_p, other_p,
    )
    return gas_next, moved.reshape(3, 1, 1, owner_count, capacity)


def solution(mesh):
    return jax.shard_map(
        per_device,
        mesh=mesh,
        in_specs=(
            P(None, "tile", None, "slab"),
            P("tile", None, "slab"),
            P(None, "tile", "slab", None),
            P("tile", "slab", None),
            P("tile", "slab", None),
            P("tile", "slab", None),
            P("tile", "slab", None, None),
            P("tile", "slab", None),
            P("tile", "slab"),
        ),
        out_specs=(P(None, "tile", None, "slab"), P(None, "tile", "slab", None, None)),
        check_vma=False,
    )
```

time: 2200 us -> 112 us (0.05)
  other arithmetic: 1210 us -> 0.02 us
  local copies, waits for them, and re-layouts: 824 us -> 5.53 us
  starting transfers between devices: 109 us -> 35.4 us
  Pallas kernels: 0 us -> 52.3 us
    scatter-add x6 -> x0, other arithmetic: 1160 us -> none  [the longest x1 319 us: per_device(): deposit.at[:, center_index - plane_size].add(kicked * weight_low[None, :])]
    gather x4 -> x0, local copies, waits for them, and re-layouts: 562 us -> none  [the longest x1 202 us: per_device(): placed = lax.iota(jnp.int32, slot_count) - firsts[sorted_owner]]
    scatter x2 -> x0, local copies, waits for them, and re-layouts: 210 us -> none  [the longest x1 120 us: per_device(): ranking = jnp.zeros((slot_count,), jnp.int32).at[ordering].set(placed)]
    ppermute x6 -> x8, starting transfers between devices: 97.4 us -> 17 us  [the longest x1 6.69 us: per_device(): right_other = lax.ppermute(dep[2, 0], ('tile', 'slab'), diagonal(to_left))]
    pallas_call x0 -> x3, Pallas kernels: none -> 52.3 us  [the longest x1 27.2 us: dispatch(): pl.pallas_call(dispatch_kernel, grid=(rows // ROWS,), in_specs=[pl.BlockS...]
    mul x2 -> x0, other arithmetic: 26.9 us -> none  [the longest x1 25.2 us: per_device(): kicked = (masses * rates)[None, :] * (speeds - gas_speed)]
  transfers between devices with their start and end apart: 7 -> 9, of which waited for: 6 -> 3; matrix products, arithmetic and copies ran while one was open for 0% -> 0% of each run, Pallas kernels for 0% -> 22%
where the time goes in v1:
time: 112 us; the launch traced here: 111 us
  Pallas kernels  52.3 us (47%)
  starting transfers between devices  35.4 us (32%)
  waiting for transfers between devices  16.7 us (15%)
  local copies, waits for them, and re-layouts  5.53 us (5%)
  between operations  1.39 us (1%)
    pallas_call x1, Pallas kernels, dispatch(): pl.pallas_call(dispatch_kernel, grid=(rows // ROWS,), in_specs=[pl.BlockS...  27.2 us
    pallas_call x1, Pallas kernels, deposit(): pl.pallas_call(deposit_kernel, grid=(count // SOURCES,), in_specs=[pl.Blo...  24.2 us
    all_to_all x1, starting transfers between devices, per_device(): lax.all_to_all(outbox.reshape(owner_count, 1, FIELDS * capacity), ('tile'...  18.4 us
    all_to_all x1, waiting for transfers between devices, per_device(): lax.all_to_all(outbox.reshape(owner_count, 1, FIELDS * capacity), ('tile'...  15.1 us
    ppermute x1, starting transfers between devices, per_device(): right_other = lax.ppermute(dep[2, 0], ('tile', 'slab'), diagonal(to_left))  6.69 us
    ppermute x1, starting transfers between devices, per_device(): right_p = lax.ppermute(pressure[:2], 'tile', to_left)  6.42 us
    unnamed x16, local copies, waits for them, and re-layouts  5.51 us
  transfers between devices with their start and end apart: 9, of which 3 were waited for; matrix products, arithmetic and copies ran while one was open for 0% of the time, Pallas kernels for 22%

profile of v1, /device:TPU:0, one launch (start us, length us, event | category | flops | bytes accessed | tf_op | source)
XLA Modules:
  0.0 111.3 jit_solution(14334618842208217498)
XLA Ops:
  1.3 1.0 copy-done.1
  2.3 0.9 copy-done.3
  3.2 0.9 copy-done.4
  4.1 0.9 copy-done.5
  5.0 0.9 copy-done.6
  5.9 0.9 copy-done.7
  6.8 27.2 %dispatch.1 = f32[2688,128]{1,0:T(8,128)} custom-call(s32[1,1]{1,0:T(1,128)S(6)} %copy.20.live_ref, f32[3,256,128]{2,1,0:T(8,128)S(1)} %bitcast.29, f32[256,128]{1,0:T(8,128)S(1)} %bitcast.30, f32[256,128]{1,0:T(8,128)S(1)} %bitcast.31, f32[256,128]{1,0:T(8,128)S(1)} %bitcast.32, s32[256,128]{1,0:T(8,128)S(1)} %bitcast.33, s32[256,128]{1,0:T(8,128)S(1)} %bitcast.34), custom_call_target="tpu_custom_call" | custom-call | tf_op jit(solution)/shard_map/dispatch/pallas_call | solution.py:156
  34.0 18.4 %all-to-all-start = ((f32[128,1,2688]{2,1,0:T(1,128)}), f32[128,1,2688]{2,1,0:T(1,128)S(1)}, u32[]{:S(2)}, u32[]{:S(2)}) async-start(f32[128,1,2688]{2,1,0:T(1,128)} %bitcast.7), calls=%async_computation | async-start | bytes 2752512 | tf_op jit(solution)/shard_map/all_to_all | solution.py:427
  52.5 0.1 collective-permute-start.7
  52.6 1.1 collective-permute-start.5
  53.7 6.4 %collective-permute-start.6 = (f32[2,16,128]{2,1,0:T(8,128)S(1)}, f32[2,16,128]{2,1,0:T(8,128)S(1)}, u32[]{:S(2)}, u32[]{:S(2)}) collective-permute-start(f32[2,16,128]{2,1,0:T(8,128)S(1)} %get-tuple-element.16), channel_id=1, source_target_pairs={{0,126},{2,0},{4,2},{6,4},{8,6},{10,8},{12,10},{14,12},{16,14},{18... | collective-permute-start | bytes 49160 | tf_op jit(solution)/shard_map/ppermute | solution.py:413
  60.1 15.1 %all-to-all-done = f32[128,1,2688]{2,1,0:T(1,128)S(1)} async-done(((f32[128,1,2688]{2,1,0:T(1,128)}), f32[128,1,2688]{2,1,0:T(1,128)S(1)}, u32[]{:S(2)}, u32[]{:S(2)}) %all-to-all-start) | async-done | bytes 1376288 | tf_op jit(solution)/shard_map/all_to_all | solution.py:427
  75.2 24.2 %deposit.1 = (f32[3,128,384]{2,1,0:T(8,128)}, f32[3,6,16,128]{3,2,1,0:T(8,128)S(1)}) custom-call(f32[2688,128]{1,0:T(8,128)S(1)} %bitcast.28, f32[4,4,16,128]{3,2,1,0:T(8,128)S(1)} %copy-done), custom_call_target="tpu_custom_call" | custom-call | tf_op jit(solution)/shard_map/deposit/pallas_call | solution.py:290
  99.5 1.5 %collective-permute-start.1 = (f32[5,16,128]{2,1,0:T(8,128)S(1)}, f32[5,16,128]{2,1,0:T(8,128)S(1)}, u32[]{:S(2)}, u32[]{:S(2)}) collective-permute-start(f32[5,16,128]{2,1,0:T(8,128)S(1)} %pad_maximum_fusion.1), channel_id=1, source_target_pairs={{0,126},{2,0},{4,2},{6,4},{8,6},{10,8},{12,10},{14,12},{16,14},{18... | collective-permute-start | bytes 122888 | tf_op jit(solution)/shard_map/ppermute | solution.py:437
  100.9 0.6 collective-permute-start
  101.6 0.0 collective-permute-done.5.left_p_ref
  101.6 0.0 collective-permute-start.2
  101.6 0.0 collective-permute-done.6.right_p_ref
  101.6 0.6 collective-permute-start.3
  102.2 0.0 collective-permute-done.7.other_p_ref
  102.2 6.7 %collective-permute-start.4 = (f32[16,128]{1,0:T(8,128)S(1)}, f32[16,128]{1,0:T(8,128)S(1)}, u32[]{:S(2)}, u32[]{:S(2)}) collective-permute-start(f32[16,128]{1,0:T(8,128)S(1)} %get-tuple-element.12), channel_id=1, source_target_pairs={{0,127},{1,126},{2,1},{3,0},{4,3},{5,2},{6,5},{7,4},{8,7},{9,6},{1... | collective-permute-start | bytes 24584 | tf_op jit(solution)/shard_map/ppermute | solution.py:440
  108.8 1.4 %collective-permute-done.3.left_other_ref = f32[16,128]{1,0:T(8,128)S(1)} collective-permute-done((f32[16,128]{1,0:T(8,128)S(1)}, f32[16,128]{1,0:T(8,128)S(1)}, u32[]{:S(2)}, u32[]{:S(2)}) %collective-permute-start.3) | collective-permute-done | bytes 8224 | tf_op jit(solution)/shard_map/ppermute | solution.py:439
  110.3 0.2 collective-permute-done.left_ref
  110.5 0.9 gas_step.1
  (21 shorter events, 0.1 us)
Async XLA Ops:
  1.3 1.0 copy-start.1
  2.3 0.9 copy-start.3
  3.2 0.9 copy-start.4
  4.1 0.9 copy-start.5
  5.0 0.9 copy-start.6
  5.9 0.9 copy-start.7
  34.0 18.4 %copy-start = (f32[4,4,16,128]{3,2,1,0:T(8,128)S(1)}, f32[4,4,16,128]{3,2,1,0:T(8,128)}, u32[]{:S(2)}) copy-start(f32[4,4,16,128]{3,2,1,0:T(8,128)} %gas_ref.3) | copy-start | bytes 393220
  34.0 18.4 %copy-start.2 = (f32[4,16,128]{2,1,0:T(8,128)S(1)}, f32[4,16,128]{2,1,0:T(8,128)}, u32[]{:S(2)}) copy-start(f32[4,16,128]{2,1,0:T(8,128)} %sound_ref.1) | copy-start | bytes 98308
  34.0 41.2 %all-to-all-start = ((f32[128,1,2688]{2,1,0:T(1,128)}), f32[128,1,2688]{2,1,0:T(1,128)S(1)}, u32[]{:S(2)}, u32[]{:S(2)}) async-start(f32[128,1,2688]{2,1,0:T(1,128)} %bitcast.7), calls=%async_computation | async-start | bytes 2752512 | tf_op jit(solution)/shard_map/all_to_all | solution.py:427
  52.5 49.7 %collective-permute-start.7 = (f32[4,16,128]{2,1,0:T(8,128)S(1)}, f32[4,16,128]{2,1,0:T(8,128)S(1)}, u32[]{:S(2)}, u32[]{:S(2)}) collective-permute-start(f32[4,16,128]{2,1,0:T(8,128)S(1)} %bitcast_multiply_fusion), channel_id=1, source_target_pairs={{0,1},{1,0},{2,3},{3,2},{4,5},{5,4},{6,7},{7,6},{8,9},{9,8},{10,11... | collective-permute-start | bytes 98312 | tf_op jit(solution)/shard_map/ppermute | solution.py:414
  52.6 49.0 %collective-permute-start.5 = (f32[2,16,128]{2,1,0:T(8,128)S(1)}, f32[2,16,128]{2,1,0:T(8,128)S(1)}, u32[]{:S(2)}, u32[]{:S(2)}) collective-permute-start(f32[2,16,128]{2,1,0:T(8,128)S(1)} %get-tuple-element.17), channel_id=1, source_target_pairs={{0,2},{2,4},{4,6},{6,8},{8,10},{10,12},{12,14},{14,16},{16,18},{18... | collective-permute-start | bytes 49160 | tf_op jit(solution)/shard_map/ppermute | solution.py:412
  53.7 47.9 %collective-permute-start.6 = (f32[2,16,128]{2,1,0:T(8,128)S(1)}, f32[2,16,128]{2,1,0:T(8,128)S(1)}, u32[]{:S(2)}, u32[]{:S(2)}) collective-permute-start(f32[2,16,128]{2,1,0:T(8,128)S(1)} %get-tuple-element.16), channel_id=1, source_target_pairs={{0,126},{2,0},{4,2},{6,4},{8,6},{10,8},{12,10},{14,12},{16,14},{18... | collective-permute-start | bytes 49160 | tf_op jit(solution)/shard_map/ppermute | solution.py:413
  99.5 10.8 %collective-permute-start.1 = (f32[5,16,128]{2,1,0:T(8,128)S(1)}, f32[5,16,128]{2,1,0:T(8,128)S(1)}, u32[]{:S(2)}, u32[]{:S(2)}) collective-permute-start(f32[5,16,128]{2,1,0:T(8,128)S(1)} %pad_maximum_fusion.1), channel_id=1, source_target_pairs={{0,126},{2,0},{4,2},{6,4},{8,6},{10,8},{12,10},{14,12},{16,14},{18... | collective-permute-start | bytes 122888 | tf_op jit(solution)/shard_map/ppermute | solution.py:437
  100.9 9.5 %collective-permute-start = (f32[5,16,128]{2,1,0:T(8,128)S(1)}, f32[5,16,128]{2,1,0:T(8,128)S(1)}, u32[]{:S(2)}, u32[]{:S(2)}) collective-permute-start(f32[5,16,128]{2,1,0:T(8,128)S(1)} %pad_maximum_fusion), channel_id=1, source_target_pairs={{0,2},{2,4},{4,6},{6,8},{8,10},{10,12},{12,14},{14,16},{16,18},{18... | collective-permute-start | bytes 122888 | tf_op jit(solution)/shard_map/ppermute | solution.py:434
  101.6 8.7 %collective-permute-start.2 = (f32[4,16,128]{2,1,0:T(8,128)S(1)}, f32[4,16,128]{2,1,0:T(8,128)S(1)}, u32[]{:S(2)}, u32[]{:S(2)}) collective-permute-start(f32[4,16,128]{2,1,0:T(8,128)S(1)} %get-tuple-element.10), channel_id=1, source_target_pairs={{0,1},{1,0},{2,3},{3,2},{4,5},{5,4},{6,7},{7,6},{8,9},{9,8},{10,11... | collective-permute-start | bytes 98312 | tf_op jit(solution)/shard_map/ppermute | solution.py:438
  101.6 8.7 %collective-permute-start.3 = (f32[16,128]{1,0:T(8,128)S(1)}, f32[16,128]{1,0:T(8,128)S(1)}, u32[]{:S(2)}, u32[]{:S(2)}) collective-permute-start(f32[16,128]{1,0:T(8,128)S(1)} %get-tuple-element.13), channel_id=1, source_target_pairs={{0,3},{1,2},{2,5},{3,4},{4,7},{5,6},{6,9},{7,8},{8,11},{9,10},{10,... | collective-permute-start | bytes 24584 | tf_op jit(solution)/shard_map/ppermute | solution.py:439
  102.2 8.1 %collective-permute-start.4 = (f32[16,128]{1,0:T(8,128)S(1)}, f32[16,128]{1,0:T(8,128)S(1)}, u32[]{:S(2)}, u32[]{:S(2)}) collective-permute-start(f32[16,128]{1,0:T(8,128)S(1)} %get-tuple-element.12), channel_id=1, source_target_pairs={{0,127},{1,126},{2,1},{3,0},{4,3},{5,2},{6,5},{7,4},{8,7},{9,6},{1... | collective-permute-start | bytes 24584 | tf_op jit(solution)/shard_map/ppermute | solution.py:440

commit v2 on v1

v2 whole, which is shorter than its diff:
```python
import jax
import jax.numpy as jnp
from jax import lax
from jax.experimental import pallas as pl
from jax.experimental.pallas import tpu as pltpu
from jax.sharding import PartitionSpec as P

courant = 0.4
LANES = 128
COLUMNS = 256
RES = 64
ROWS = 16
SOURCES = 8
FIELDS = 7
VMEM_BYTES = 40 * 1024 * 1024
NT = (((1,), (1,)), ((), ()))
NN = (((1,), (0,)), ((), ()))


def split2(x):
    hi = x.astype(jnp.bfloat16).astype(jnp.float32)
    return hi, x - hi


def dispatch_kernel(
    live_ref, vel_ref, rate_ref, mass_ref, off_ref, owner_ref, cell_ref, out_ref,
    acc, values, lead0, lead1, onehot0, onehot1, spare, owners, base, pending, combined,
):
    owner_count = base.shape[0]
    windows = acc.shape[1]
    groups = acc.shape[2]
    pitch = out_ref.shape[0] // owner_count
    chunk = ROWS * LANES
    width = FIELDS * groups
    step = pl.program_id(0)
    f32, bf16 = jnp.float32, jnp.bfloat16
    leads = (lead0, lead1)
    onehots = (onehot0, onehot1)

    @pl.when(step == 0)
    def _():
        acc[...] = jnp.zeros_like(acc)
        base[...] = jnp.zeros_like(base)
        pending[...] = jnp.full_like(pending, -65536.0)

    def short_iota(rows):
        return lax.broadcasted_iota(jnp.int32, (rows, LANES), 0).astype(f32).astype(bf16)

    def short_rows(row):
        return jnp.broadcast_to(row, (16, LANES)).astype(bf16)

    one = jnp.ones((16, LANES), bf16)
    zero = jnp.zeros((16, LANES), bf16)

    def spread(target, row, cols, rows):
        same = short_rows(row)
        numbers = short_iota(rows)
        for b in range(rows // 16):
            block = slice(b * 16, (b + 1) * 16)
            target[block, cols] = jnp.where(same == numbers[block], one, zero)

    def write_onehot(target, picked):
        for j in range(ROWS):
            spread(target, picked[j : j + 1, :], slice(j * LANES, (j + 1) * LANES), COLUMNS)

    def add_product(lead, onehot, start, number):
        product = lax.dot_general(lead[...], onehot[...], NT, preferred_element_type=f32)
        product = product[:width] + product[width:]
        starts = start.astype(jnp.int32)
        lane = lax.broadcasted_iota(jnp.int32, (groups, LANES), 1)
        for k in range(COLUMNS // LANES):
            cols = slice(k * LANES, (k + 1) * LANES)
            even = starts[2 * k * groups : (2 * k + 1) * groups]
            odd = starts[(2 * k + 1) * groups : (2 * k + 2) * groups]
            first = jnp.where(lane < RES, even, odd) + number * RES
            window = (first + (((lane & (RES - 1)) - first) & (RES - 1))) >> 6
            for w in range(windows):
                here = window == w
                for v in range(FIELDS):
                    acc[v, w, :, cols] += jnp.where(
                        here, product[v * groups : (v + 1) * groups, cols], 0.0
                    )

    def build(h):
        part = slice(h * ROWS, (h + 1) * ROWS)
        lead, onehot = leads[h], onehots[h]
        slot = (
            (2 * step + h) * chunk
            + lax.broadcasted_iota(jnp.int32, (ROWS, LANES), 0) * LANES
            + lax.broadcasted_iota(jnp.int32, (ROWS, LANES), 1)
        )
        alive = slot < live_ref[0, 0]
        dest = jnp.where(alive, owner_ref[part], owner_count)
        destf = dest.astype(f32)

        for j in range(ROWS):
            t, half = j // 2, j % 2
            spread(
                owners.at[t * owner_count : (t + 1) * owner_count],
                destf[j : j + 1, :], slice(half * LANES, (half + 1) * LANES), owner_count,
            )
        before = lax.broadcasted_iota(jnp.int32, (COLUMNS, COLUMNS + LANES), 0)
        after = lax.broadcasted_iota(jnp.int32, (COLUMNS, COLUMNS + LANES), 1)
        upper = jnp.where(before < after, 1.0, 0.0).astype(bf16)
        prior = lax.dot_general(owners[...], upper, NN, preferred_element_type=f32)
        owner_row = lax.broadcasted_iota(jnp.int32, (owner_count, LANES), 0)
        start = base[...]
        running = start * float(chunk)
        for t in range(ROWS // 2):
            rows = slice(t * owner_count, (t + 1) * owner_count)
            for half in range(2):
                j = 2 * t + half
                total = prior[rows, half * LANES : (half + 1) * LANES] + running
                combined[j : j + 1, :] = jnp.sum(
                    jnp.where(dest[j : j + 1, :] == owner_row, total, 0.0), axis=0, keepdims=True
                )
            running = running + prior[rows, COLUMNS:]
        tally = running - start * float(chunk)
        base[...] = start + tally
        pending[h] = start
        both = combined[...].astype(jnp.int32)
        local_rank = both & (chunk - 1)
        rank = local_rank + (both >> 11)
        column = (dest // groups) * RES + (rank & (RES - 1))
        turn = jnp.where(alive, local_rank >> 6, -1)

        fields = [
            vel_ref[0, part], vel_ref[1, part], vel_ref[2, part], rate_ref[part], mass_ref[part],
            off_ref[part], cell_ref[part].astype(f32),
        ]
        for v, field in enumerate(fields):
            hi, lo = split2(field)
            values[v] = hi
            values[v + FIELDS] = lo
        group = (dest & (groups - 1)).astype(f32)
        numbers = short_iota(groups)
        for j in range(ROWS):
            same = short_rows(group[j : j + 1, :])
            masks = [same == numbers[b * 16 : (b + 1) * 16] for b in range(groups // 16)]
            for v in range(2 * FIELDS):
                value = short_rows(values[v, j : j + 1, :])
                for b, mask in enumerate(masks):
                    at = v * groups + b * 16
                    lead[at : at + 16, j * LANES : (j + 1) * LANES] = jnp.where(mask, value, zero)
        write_onehot(onehot, jnp.where(turn == 0, column, -1).astype(f32))
        passes = (jnp.max(tally).astype(jnp.int32) + RES - 1) >> 6
        return passes, turn, column, start

    def further(h, state):
        passes, turn, column, start = state

        @pl.when(passes > 1)
        def _():
            def one_pass(number, carry):
                write_onehot(spare, jnp.where(turn == number, column, -1).astype(f32))
                add_product(leads[h], spare, start, number)
                return carry

            lax.fori_loop(1, passes, one_pass, 0)

    late = pending[1]
    states = [build(0)]
    add_product(lead1, onehot1, late, 0)
    states.append(build(1))
    add_product(lead0, onehot0, pending[0], 0)
    for h in range(2):
        further(h, states[h])

    @pl.when(step == pl.num_programs(0) - 1)
    def _():
        add_product(lead1, onehot1, pending[1], 0)
        low = lax.broadcasted_iota(jnp.int32, (8, LANES), 1) < RES
        for v in range(FIELDS):
            for k in range(COLUMNS // LANES):
                cols = slice(k * LANES, (k + 1) * LANES)
                for m in range(windows // 2):
                    for part in range(groups // 8):
                        rows = slice(part * 8, (part + 1) * 8)
                        near = acc[v, 2 * m, rows, cols]
                        far = acc[v, 2 * m + 1, rows, cols]
                        place = v * (windows // 2) + m
                        even = (2 * k * groups + part * 8) * pitch + place
                        odd = ((2 * k + 1) * groups + part * 8) * pitch + place
                        out_ref[pl.ds(even, 8, stride=pitch), :] = jnp.where(
                            low, near, pltpu.roll(far, RES, 1)
                        )
                        out_ref[pl.ds(odd, 8, stride=pitch), :] = jnp.where(
                            low, pltpu.roll(near, RES, 1), far
                        )


def dispatch(live, vel, rate, mass, off, owner, cell, owner_count, capacity):
    rows = rate.shape[0]
    groups = owner_count * RES // COLUMNS
    chunk = ROWS * LANES
    pitch = FIELDS * capacity // LANES
    plain = pl.BlockSpec((2 * ROWS, LANES), lambda i: (i, 0))
    lead = pltpu.VMEM((2 * FIELDS * groups, chunk), jnp.bfloat16)
    onehot = pltpu.VMEM((COLUMNS, chunk), jnp.bfloat16)
    return pl.pallas_call(
        dispatch_kernel,
        grid=(rows // (2 * ROWS),),
        in_specs=[
            pl.BlockSpec(memory_space=pltpu.SMEM),
            pl.BlockSpec((3, 2 * ROWS, LANES), lambda i: (0, i, 0)),
            plain, plain, plain, plain, plain,
        ],
        out_specs=pl.BlockSpec((owner_count * pitch, LANES), lambda i: (0, 0)),
        out_shape=jax.ShapeDtypeStruct((owner_count * pitch, LANES), jnp.float32),
        scratch_shapes=[
            pltpu.VMEM((FIELDS, capacity // RES, groups, COLUMNS), jnp.float32),
            pltpu.VMEM((2 * FIELDS, ROWS, LANES), jnp.float32),
            lead, lead, onehot, onehot, onehot,
            pltpu.VMEM((ROWS // 2 * owner_count, COLUMNS), jnp.bfloat16),
            pltpu.VMEM((owner_count, LANES), jnp.float32),
            pltpu.VMEM((2, owner_count, LANES), jnp.float32),
            pltpu.VMEM((ROWS, LANES), jnp.float32),
        ],
        compiler_params=pltpu.CompilerParams(vmem_limit_bytes=60 * 1024 * 1024),
        name="dispatch",
    )(live, vel, rate, mass, off, owner, cell)


def deposit_kernel(
    arrived_ref, gas_ref, sound_ref,
    moved_ref, raw_ref, to_right_ref, to_left_ref, to_other_ref,
    table, total, onehot0, onehot1, lead0, lead1, speeds, pieces,
):
    capacity = moved_ref.shape[2]
    width_x = gas_ref.shape[1]
    reach = width_x + 2
    strips = 8
    rows = width_x * strips
    half = 3 * reach * strips
    pitch = arrived_ref.shape[0] // (2 * SOURCES)
    parts = capacity // LANES
    f32, bf16 = jnp.float32, jnp.bfloat16
    step = pl.program_id(0)
    leads = (lead0, lead1)
    onehots = (onehot0, onehot1)

    @pl.when(step == 0)
    def _():
        total[...] = jnp.zeros_like(total)
        for v in range(3):
            for x in range(0, width_x, 2):
                for h in range(2):
                    two = [gas_ref[1 + v, x + i, h * 8 : (h + 1) * 8, :] for i in range(2)]
                    hi, lo = split2(jnp.concatenate(two, axis=0))
                    at = v * rows + x * strips
                    cols = slice(h * LANES, (h + 1) * LANES)
                    table[at : at + 16, cols] = hi.astype(bf16)
                    table[3 * rows + at : 3 * rows + at + 16, cols] = lo.astype(bf16)

    one = jnp.ones((16, capacity), bf16)
    zero = jnp.zeros((16, capacity), bf16)
    number = lax.broadcasted_iota(jnp.int32, (16, capacity), 0)
    numbers = [(number + 16 * b).astype(f32).astype(bf16) for b in range(COLUMNS // 16)]
    strip_number = (number & (strips - 1)).astype(f32).astype(bf16)
    row_row = lax.broadcasted_iota(jnp.int32, (rows, capacity), 0)

    def short_rows(row):
        return jnp.broadcast_to(row, (16, capacity)).astype(bf16)

    def spans(s):
        return slice(s * capacity, (s + 1) * capacity)

    def field(h, v):
        first = h * SOURCES * pitch + v * parts
        return jnp.concatenate(
            [arrived_ref[pl.ds(first + m, SOURCES, stride=pitch), :] for m in range(parts)], axis=1
        )

    def look_up(h):
        cell = field(h, 6).astype(jnp.int32)
        column = ((cell & (LANES - 1)) + ((cell >> 10) & 1) * LANES).astype(f32)
        for s in range(SOURCES):
            same = short_rows(column[s : s + 1, :])
            for b in range(COLUMNS // 16):
                onehots[h][b * 16 : (b + 1) * 16, spans(s)] = jnp.where(
                    same == numbers[b], one, zero
                )
        found = lax.dot_general(table[...], onehots[h][...], NN, preferred_element_type=f32)
        return cell, found[: 3 * rows] + found[3 * rows :]

    def relax(h, cell, found):
        part = slice(h * SOURCES, (h + 1) * SOURCES)
        plane = cell >> 11
        strip = (cell >> 7) & (strips - 1)
        row = plane * strips + strip
        for s in range(SOURCES):
            mask = row[s : s + 1, :] == row_row
            for v in range(3):
                speeds[v, s : s + 1, :] = jnp.sum(
                    jnp.where(mask, found[v * rows : (v + 1) * rows, spans(s)], 0.0),
                    axis=0, keepdims=True,
                )
        rate = field(h, 3)
        mass = field(h, 4)
        shift = field(h, 5)
        occupied = mass > 0.0
        low_weight = 0.5 * (0.5 - shift) ** 2
        mid_weight = 0.75 - shift**2
        high_weight = 0.5 * (0.5 + shift) ** 2
        weights = []
        for x in range(reach):
            rest = jnp.where(plane == x - 2, high_weight, 0.0)
            rest = jnp.where(plane == x - 1, mid_weight, rest)
            weights.append(jnp.where(plane == x, low_weight, rest))
        for v in range(3):
            speed = field(h, v)
            slip = speed - speeds[v]
            moved_ref[v, part] = jnp.where(occupied, speed - rate * slip, 0.0)
            kick = mass * rate * slip
            for x in range(reach):
                hi, lo = split2(kick * weights[x])
                pieces[v * reach + x] = hi
                pieces[(3 + v) * reach + x] = lo
        stripf = strip.astype(f32)
        for s in range(SOURCES):
            mask = short_rows(stripf[s : s + 1, :]) == strip_number
            for pair in range(3 * reach):
                both = [
                    jnp.broadcast_to(pieces[2 * pair + i, s : s + 1, :], (strips, capacity))
                    for i in range(2)
                ]
                leads[h][pair * 16 : (pair + 1) * 16, spans(s)] = jnp.where(
                    mask, jnp.concatenate(both, axis=0).astype(bf16), zero
                )

    def gather_up(h, keep):
        product = lax.dot_general(leads[h][...], onehots[h][...], NT, preferred_element_type=f32)
        product = product[:half] + product[half:]
        if keep is not None:
            product = jnp.where(keep, product, 0.0)
        total[...] = total[...] + product

    found = look_up(0)
    gather_up(1, step > 0)
    relax(0, *found)
    found = look_up(1)
    gather_up(0, None)
    relax(1, *found)

    @pl.when(step == pl.num_programs(0) - 1)
    def _():
        gather_up(1, None)

        def added(v, x):
            at = (v * reach + x) * strips
            return jnp.concatenate(
                [total[at : at + strips, h * LANES : (h + 1) * LANES] for h in range(2)], axis=0
            )

        for v in range(3):
            to_left_ref[4 + v] = added(v, 0)
            to_right_ref[4 + v] = added(v, width_x + 1)
            for x in range(width_x):
                raw_ref[v, x] = gas_ref[1 + v, x] + added(v, x + 1)
        to_other_ref[2 * width_x] = added(2, 0)
        to_other_ref[2 * width_x + 1] = added(2, width_x + 1)
        for x in range(width_x):
            pressure = sound_ref[x] * gas_ref[0, x]
            to_other_ref[x] = raw_ref[2, x]
            to_other_ref[width_x + x] = pressure
            if x < 2:
                to_left_ref[x] = pressure
                to_left_ref[2 + x] = raw_ref[0, x]
            if x >= width_x - 2:
                to_right_ref[x - width_x + 2] = pressure
                to_right_ref[x - width_x + 4] = raw_ref[0, x]


def deposit(arrived, gas, sound, count, capacity):
    pitch = arrived.shape[0] // count
    width_x, width_y, width_z = gas.shape[1:]
    reach = width_x + 2
    deposit_rows = 3 * reach * 8
    plane = (width_y, width_z)
    shapes = [(3, width_x) + plane, (7,) + plane, (7,) + plane, (2 * width_x + 2,) + plane]

    def whole(shape):
        return pl.BlockSpec(shape, lambda i: (0,) * len(shape))

    onehot = pltpu.VMEM((COLUMNS, SOURCES * capacity), jnp.bfloat16)
    lead = pltpu.VMEM((2 * deposit_rows, SOURCES * capacity), jnp.bfloat16)
    return pl.pallas_call(
        deposit_kernel,
        grid=(count // (2 * SOURCES),),
        in_specs=[
            pl.BlockSpec((2 * SOURCES * pitch, LANES), lambda i: (i, 0)),
            whole(gas.shape),
            whole(sound.shape),
        ],
        out_specs=[pl.BlockSpec((3, 2 * SOURCES, capacity), lambda i: (0, i, 0))]
        + [whole(shape) for shape in shapes],
        out_shape=[
            jax.ShapeDtypeStruct(shape, jnp.float32) for shape in [(3, count, capacity)] + shapes
        ],
        scratch_shapes=[
            pltpu.VMEM((6 * width_x * 8, COLUMNS), jnp.bfloat16),
            pltpu.VMEM((deposit_rows, COLUMNS), jnp.float32),
            onehot, onehot, lead, lead,
            pltpu.VMEM((3, SOURCES, capacity), jnp.float32),
            pltpu.VMEM((6 * reach, SOURCES, capacity), jnp.float32),
        ],
        compiler_params=pltpu.CompilerParams(vmem_limit_bytes=VMEM_BYTES),
        name="deposit",
    )(arrived, gas, sound)


def step_kernel(
    slab_ref, gas_ref, sound_ref, raw_ref, mine_left_ref, mine_right_ref,
    left_ref, right_ref, other_ref, next_ref,
):
    width_x, width_y, width_z = sound_ref.shape
    slab = slab_ref[0, 0]
    first_slab = slab == 0
    lane = lax.broadcasted_iota(jnp.int32, (width_y, width_z), 1)

    def along_y(f, shift):
        return pltpu.roll(f, (-shift) % width_y, 0)

    def along_z(f, other, shift):
        turned = pltpu.roll(f, (-shift) % width_z, 1)
        beyond = pltpu.roll(other, (-shift) % width_z, 1)
        if shift > 0:
            inside = lane < width_z - shift
            reached = first_slab
        else:
            inside = lane >= -shift
            reached = jnp.logical_not(first_slab)
        return jnp.where(inside, turned, jnp.where(reached, beyond, 0.0))

    def fourth(shifted):
        return (8.0 * (shifted(1) - shifted(-1)) - (shifted(2) - shifted(-2))) / 12.0

    def momentum(k, x):
        value = raw_ref[k, x]
        if x == 0:
            value = value + left_ref[4 + k]
        if x == width_x - 1:
            value = value + right_ref[4 + k]
        return value

    planes = [[momentum(k, x) for x in range(width_x)] for k in range(3)]
    first = {x: planes[0][x] for x in range(width_x)}
    first[-2] = left_ref[2]
    first[-1] = left_ref[3] + mine_left_ref[4]
    first[width_x] = right_ref[2] + mine_right_ref[4]
    first[width_x + 1] = right_ref[3]
    pressure = {x: sound_ref[x] * gas_ref[0, x] for x in range(width_x)}
    pressure[-2] = left_ref[0]
    pressure[-1] = left_ref[1]
    pressure[width_x] = right_ref[0]
    pressure[width_x + 1] = right_ref[1]
    for x in range(width_x):
        other = other_ref[x]
        if x == 0:
            other = other + left_ref[7]
        if x == width_x - 1:
            other = other + right_ref[7]
        other_p = other_ref[width_x + x]
        p = pressure[x]
        next_ref[0, x] = gas_ref[0, x] - courant * (
            fourth(lambda s: first[x + s])
            + fourth(lambda s: along_y(planes[1][x], s))
            + fourth(lambda s: along_z(planes[2][x], other, s))
        )
        next_ref[1, x] = planes[0][x] - courant * fourth(lambda s: pressure[x + s])
        next_ref[2, x] = planes[1][x] - courant * fourth(lambda s: along_y(p, s))
        next_ref[3, x] = planes[2][x] - courant * fourth(lambda s: along_z(p, other_p, s))


def gas_step(slab, gas, *rest):
    whole = pl.BlockSpec(memory_space=pltpu.VMEM)
    return pl.pallas_call(
        step_kernel,
        in_specs=[pl.BlockSpec(memory_space=pltpu.SMEM)] + [whole] * (1 + len(rest)),
        out_specs=whole,
        out_shape=jax.ShapeDtypeStruct(gas.shape, jnp.float32),
        compiler_params=pltpu.CompilerParams(vmem_limit_bytes=VMEM_BYTES),
        name="gas_step",
    )(slab, gas, *rest)


def per_device(
    gas_state, sound_speed, velocity, drag_rate, parcel_mass, cell_offset, target_owner,
    target_cell, live_counts,
):
    tiles = lax.axis_size("tile")
    slabs = lax.axis_size("slab")
    owner_count = tiles * slabs
    slot_count = target_cell.shape[-1]
    capacity = 3 * slot_count // (2 * owner_count)
    rows = slot_count // LANES
    width_x = gas_state.shape[1]
    to_right = [(t, (t + 1) % tiles) for t in range(tiles)]
    to_left = [(t, (t - 1) % tiles) for t in range(tiles)]
    swap = [(s, slabs - 1 - s) for s in range(slabs)]

    outbox = dispatch(
        live_counts,
        velocity.reshape(3, rows, LANES),
        drag_rate.reshape(rows, LANES),
        parcel_mass.reshape(rows, LANES),
        cell_offset.reshape(rows, LANES),
        target_owner.reshape(rows, LANES),
        target_cell.reshape(rows, LANES),
        owner_count,
        capacity,
    )
    arrived = lax.all_to_all(
        outbox.reshape(owner_count, 1, FIELDS * capacity), ("tile", "slab"),
        split_axis=0, concat_axis=0, tiled=True,
    ).reshape(outbox.shape)
    moved, raw, mine_right, mine_left, mine = deposit(
        arrived, gas_state, sound_speed, owner_count, capacity
    )
    other = lax.ppermute(mine, "slab", swap)
    left = lax.ppermute(
        jnp.concatenate([mine_right, other[2 * width_x + 1 :]]), "tile", to_right
    )
    right = lax.ppermute(
        jnp.concatenate([mine_left, other[2 * width_x : 2 * width_x + 1]]), "tile", to_left
    )
    slab = lax.axis_index("slab").astype(jnp.int32).reshape(1, 1)
    gas_next = gas_step(
        slab, gas_state, sound_speed, raw, mine_left, mine_right,
        left, right, other,
    )
    return gas_next, moved.reshape(3, 1, 1, owner_count, capacity)


def solution(mesh):
    return jax.shard_map(
        per_device,
        mesh=mesh,
        in_specs=(
            P(None, "tile", None, "slab"),
            P("tile", None, "slab"),
            P(None, "tile", "slab", None),
            P("tile", "slab", None),
            P("tile", "slab", None),
            P("tile", "slab", None),
            P("tile", "slab", None, None),
            P("tile", "slab", None),
            P("tile", "slab"),
        ),
        out_specs=(P(None, "tile", None, "slab"), P(None, "tile", "slab", None, None)),
        check_vma=False,
    )
```

time: 112 us -> 93.9 us (0.84)
  blocking collectives: 0 us -> 33.8 us
  starting transfers between devices: 35.4 us -> 2.1 us
  waiting for transfers between devices: 16.7 us -> 10.4 us
  Pallas kernels: 52.3 us -> 46.1 us
  local copies, waits for them, and re-layouts: 5.53 us -> 0.01 us
    all_to_all x0 -> x1, blocking collectives: none -> 33.8 us  [per_device(): lax.all_to_all(outbox.reshape(owner_count, 1, FIELDS * capacity), ('tile'...]
    all_to_all x1 -> x0, starting transfers between devices: 18.4 us -> none  [per_device(): lax.all_to_all(outbox.reshape(owner_count, 1, FIELDS * capacity), ('tile'...]
    all_to_all x1 -> x0, waiting for transfers between devices: 15.1 us -> none  [per_device(): lax.all_to_all(outbox.reshape(owner_count, 1, FIELDS * capacity), ('tile'...]
    ppermute x8 -> x3, starting transfers between devices: 17 us -> 2.1 us  [the longest x1 1.48 us: per_device(): lax.ppermute(jnp.concatenate([mine_left, other[2 * width_x:2 * width_x +...]
    ppermute x8 -> x3, waiting for transfers between devices: 1.61 us -> 10.4 us  [the longest x1 6.85 us: per_device(): lax.ppermute(jnp.concatenate([mine_right, other[2 * width_x + 1:]]), 'til...]
    pallas_call x2, Pallas kernels: 51.4 us -> 45.3 us  [the longest x1 25.6 us: dispatch(): pl.pallas_call(dispatch_kernel, grid=(rows // (2 * ROWS),), in_specs=[pl....]
    unnamed x16 -> x4, local copies, waits for them, and re-layouts: 5.51 us -> 0.01 us
  transfers between devices with their start and end apart: 9 -> 3, of which waited for: 3 -> 3; matrix products, arithmetic and copies ran while one was open for 0% -> 0% of each run, Pallas kernels for 22% -> 0%
where the time goes in v2:
time: 93.9 us; the launch traced here: 93.7 us
  Pallas kernels  46.1 us (49%)
  blocking collectives  33.8 us (36%)
  waiting for transfers between devices  10.4 us (11%)
  starting transfers between devices  2.1 us (2%)
  between operations  1.29 us (1%)
    all_to_all x1, blocking collectives, per_device(): lax.all_to_all(outbox.reshape(owner_count, 1, FIELDS * capacity), ('tile'...  33.8 us
    pallas_call x1, Pallas kernels, dispatch(): pl.pallas_call(dispatch_kernel, grid=(rows // (2 * ROWS),), in_specs=[pl....  25.6 us
    pallas_call x1, Pallas kernels, deposit(): pl.pallas_call(deposit_kernel, grid=(count // (2 * SOURCES),), in_specs=[...  19.7 us
    ppermute x1, waiting for transfers between devices, per_device(): lax.ppermute(jnp.concatenate([mine_right, other[2 * width_x + 1:]]), 'til...  6.85 us
    ppermute x1, waiting for transfers between devices, per_device(): lax.ppermute(jnp.concatenate([mine_left, other[2 * width_x:2 * width_x +...  2.23 us
  transfers between devices with their start and end apart: 3, of which 3 were waited for; matrix products, arithmetic and copies ran while one was open for 0% of the time, Pallas kernels for 0%

profile of v2, /device:TPU:0, one launch (start us, length us, event | category | flops | bytes accessed | tf_op | source)
XLA Modules:
  0.0 93.7 jit_solution(10644398398094124303)
XLA Ops:
  1.3 25.6 %dispatch.1 = f32[2688,128]{1,0:T(8,128)} custom-call(s32[1,1]{1,0:T(1,128)S(6)} %copy.14.live_ref, f32[3,256,128]{2,1,0:T(8,128)} %bitcast.14, f32[256,128]{1,0:T(8,128)} %bitcast.15, f32[256,128]{1,0:T(8,128)} %bitcast.16, f32[256,128]{1,0:T(8,128)} %bitcast.17, s32[256,128]{1,0:T(8,128)} %bitcast.18, s32[256,128]{1,0:T(8,128)} %bitcast.19), custom_call_target="tpu_custom_call" | custom-call | tf_op jit(solution)/shard_map/dispatch/pallas_call | solution.py:200
  26.9 0.0 copy-start
  26.9 0.0 copy-start.1
  26.9 33.8 %all_to_all.5 = f32[128,1,2688]{2,1,0:T(1,128)S(1)} all-to-all(f32[128,1,2688]{2,1,0:T(1,128)} %bitcast.13), channel_id=1, replica_groups=mesh['tile'=64,'slab'=2] {'tile','slab'}, dimensions={0} | all-to-all | bytes 2752512 | tf_op jit(solution)/shard_map/all_to_all | solution.py:513
  60.7 0.0 copy-done
  60.7 0.0 copy-done.1
  60.7 19.7 %deposit.1 = (f32[3,128,384]{2,1,0:T(8,128)}, f32[3,4,16,128]{3,2,1,0:T(8,128)S(1)}, f32[7,16,128]{2,1,0:T(8,128)S(1)}, f32[7,16,128]{2,1,0:T(8,128)S(1)}, f32[10,16,128]{2,1,0:T(8,128)S(1)}) custom-call(f32[2688,128]{1,0:T(8,128)S(1)} %bitcast.12, f32[4,4,16,128]{3,2,1,0:T(8,128)S(1)} %copy-done, f32[4,16,128]{2,1,0:T(8,128)S(1)} %copy-done.1), custom_call_target="tpu_custom_call" | custom-call | tf_op jit(solution)/shard_map/deposit/pallas_call | solution.py:387
  80.4 0.0 collective-permute-start
  80.4 1.3 %collective-permute-done.other_ref = f32[10,16,128]{2,1,0:T(8,128)S(1)} collective-permute-done((f32[10,16,128]{2,1,0:T(8,128)S(1)}, f32[10,16,128]{2,1,0:T(8,128)S(1)}, u32[]{:S(2)}, u32[]{:S(2)}) %collective-permute-start) | collective-permute-done | bytes 81952 | tf_op jit(solution)/shard_map/ppermute | solution.py:520
  81.7 1.5 %collective-permute-start.2 = (f32[8,16,128]{2,1,0:T(8,128)S(1)}, f32[8,16,128]{2,1,0:T(8,128)S(1)}, u32[]{:S(2)}, u32[]{:S(2)}) collective-permute-start(f32[8,16,128]{2,1,0:T(8,128)S(1)} %pad_maximum_fusion.1), channel_id=1, source_target_pairs={{0,126},{2,0},{4,2},{6,4},{8,6},{10,8},{12,10},{14,12},{16,14},{18... | collective-permute-start | bytes 196616 | tf_op jit(solution)/shard_map/ppermute | solution.py:524
  83.1 0.6 collective-permute-start.1
  83.8 2.2 %collective-permute-done.2.right_ref = f32[8,16,128]{2,1,0:T(8,128)S(1)} collective-permute-done((f32[8,16,128]{2,1,0:T(8,128)S(1)}, f32[8,16,128]{2,1,0:T(8,128)S(1)}, u32[]{:S(2)}, u32[]{:S(2)}) %collective-permute-start.2) | collective-permute-done | bytes 65568 | tf_op jit(solution)/shard_map/ppermute | solution.py:524
  86.0 6.9 %collective-permute-done.1.left_ref = f32[8,16,128]{2,1,0:T(8,128)S(1)} collective-permute-done((f32[8,16,128]{2,1,0:T(8,128)S(1)}, f32[8,16,128]{2,1,0:T(8,128)S(1)}, u32[]{:S(2)}, u32[]{:S(2)}) %collective-permute-start.1) | collective-permute-done | bytes 65568 | tf_op jit(solution)/shard_map/ppermute | solution.py:521
  92.8 0.9 gas_step.1
  (3 shorter events, 0.0 us)
Async XLA Ops:
  26.9 33.8 %copy-start = (f32[4,4,16,128]{3,2,1,0:T(8,128)S(1)}, f32[4,4,16,128]{3,2,1,0:T(8,128)}, u32[]{:S(2)}) copy-start(f32[4,4,16,128]{3,2,1,0:T(8,128)} %gas_ref.3) | copy-start | bytes 393220
  26.9 33.8 %copy-start.1 = (f32[4,16,128]{2,1,0:T(8,128)S(1)}, f32[4,16,128]{2,1,0:T(8,128)}, u32[]{:S(2)}) copy-start(f32[4,16,128]{2,1,0:T(8,128)} %sound_ref.3) | copy-start | bytes 98308
  80.4 1.3 %collective-permute-start = (f32[10,16,128]{2,1,0:T(8,128)S(1)}, f32[10,16,128]{2,1,0:T(8,128)S(1)}, u32[]{:S(2)}, u32[]{:S(2)}) collective-permute-start(f32[10,16,128]{2,1,0:T(8,128)S(1)} %get-tuple-element.10), channel_id=1, source_target_pairs={{0,1},{1,0},{2,3},{3,2},{4,5},{5,4},{6,7},{7,6},{8,9},{9,8},{10,11... | collective-permute-start | bytes 245768 | tf_op jit(solution)/shard_map/ppermute | solution.py:520
  81.7 4.3 %collective-permute-start.2 = (f32[8,16,128]{2,1,0:T(8,128)S(1)}, f32[8,16,128]{2,1,0:T(8,128)S(1)}, u32[]{:S(2)}, u32[]{:S(2)}) collective-permute-start(f32[8,16,128]{2,1,0:T(8,128)S(1)} %pad_maximum_fusion.1), channel_id=1, source_target_pairs={{0,126},{2,0},{4,2},{6,4},{8,6},{10,8},{12,10},{14,12},{16,14},{18... | collective-permute-start | bytes 196616 | tf_op jit(solution)/shard_map/ppermute | solution.py:524
  83.1 9.7 %collective-permute-start.1 = (f32[8,16,128]{2,1,0:T(8,128)S(1)}, f32[8,16,128]{2,1,0:T(8,128)S(1)}, u32[]{:S(2)}, u32[]{:S(2)}) collective-permute-start(f32[8,16,128]{2,1,0:T(8,128)S(1)} %pad_maximum_fusion), channel_id=1, source_target_pairs={{0,2},{2,4},{4,6},{6,8},{8,10},{10,12},{12,14},{14,16},{16,18},{18... | collective-permute-start | bytes 196616 | tf_op jit(solution)/shard_map/ppermute | solution.py:521

commit v3 on v2

--- a/solution.py
+++ b/solution.py
@@ -9,7 +9,9 @@
 LANES = 128
 COLUMNS = 256
 RES = 64
+CHUNKS = 4
 ROWS = 16
+BLOCKS = 4
 SOURCES = 8
 FIELDS = 7
 VMEM_BYTES = 40 * 1024 * 1024
@@ -24,7 +26,7 @@
 
 def dispatch_kernel(
     live_ref, vel_ref, rate_ref, mass_ref, off_ref, owner_ref, cell_ref, out_ref,
-    acc, values, lead0, lead1, onehot0, onehot1, spare, owners, base, pending, combined,
+    acc, values, base, combined,
 ):
     owner_count = base.shape[0]
     windows = acc.shape[1]
@@ -34,37 +36,54 @@
     width = FIELDS * groups
     step = pl.program_id(0)
     f32, bf16 = jnp.float32, jnp.bfloat16
-    leads = (lead0, lead1)
-    onehots = (onehot0, onehot1)
 
     @pl.when(step == 0)
     def _():
         acc[...] = jnp.zeros_like(acc)
         base[...] = jnp.zeros_like(base)
-        pending[...] = jnp.full_like(pending, -65536.0)
 
     def short_iota(rows):
-        return lax.broadcasted_iota(jnp.int32, (rows, LANES), 0).astype(f32).astype(bf16)
+        return lax.broadcasted_iota(jnp.int32, (rows, COLUMNS), 0).astype(f32).astype(bf16)
+
+    def pair(x, t):
+        return jnp.concatenate([x[2 * t : 2 * t + 1, :], x[2 * t + 1 : 2 * t + 2, :]], axis=1)
 
     def short_rows(row):
-        return jnp.broadcast_to(row, (16, LANES)).astype(bf16)
-
-    one = jnp.ones((16, LANES), bf16)
-    zero = jnp.zeros((16, LANES), bf16)
-
-    def spread(target, row, cols, rows):
+        return jnp.broadcast_to(row, (16, COLUMNS)).astype(bf16)
+
+    one = jnp.ones((16, COLUMNS), bf16)
+    zero = jnp.zeros((16, COLUMNS), bf16)
+
+    def spread(row, rows):
         same = short_rows(row)
         numbers = short_iota(rows)
-        for b in range(rows // 16):
-            block = slice(b * 16, (b + 1) * 16)
-            target[block, cols] = jnp.where(same == numbers[block], one, zero)
-
-    def write_onehot(target, picked):
-        for j in range(ROWS):
-            spread(target, picked[j : j + 1, :], slice(j * LANES, (j + 1) * LANES), COLUMNS)
-
-    def add_product(lead, onehot, start, number):
-        product = lax.dot_general(lead[...], onehot[...], NT, preferred_element_type=f32)
+        return jnp.concatenate(
+            [
+                jnp.where(same == numbers[b * 16 : (b + 1) * 16], one, zero)
+                for b in range(rows // 16)
+            ],
+            axis=0,
+        )
+
+    def multiply(group, picked, buffer):
+        product = None
+        numbers = short_iota(groups)
+        for t in range(ROWS // 2):
+            onehot = spread(pair(picked, t), COLUMNS)
+            same = short_rows(pair(group, t))
+            masks = [same == numbers[b * 16 : (b + 1) * 16] for b in range(groups // 16)]
+            blocks = []
+            for v in range(2 * FIELDS):
+                value = short_rows(pair(values[buffer, v], t))
+                for mask in masks:
+                    blocks.append(jnp.where(mask, value, zero))
+            part = lax.dot_general(
+                jnp.concatenate(blocks, axis=0), onehot, NT, preferred_element_type=f32
+            )
+            product = part if product is None else product + part
+        return product
+
+    def add_product(product, start, number):
         product = product[:width] + product[width:]
         starts = start.astype(jnp.int32)
         lane = lax.broadcasted_iota(jnp.int32, (groups, LANES), 1)
@@ -81,94 +100,74 @@
                         here, product[v * groups : (v + 1) * groups, cols], 0.0
                     )
 
-    def build(h):
+    before = lax.broadcasted_iota(jnp.int32, (COLUMNS, COLUMNS + LANES), 0)
+    after = lax.broadcasted_iota(jnp.int32, (COLUMNS, COLUMNS + LANES), 1)
+    upper = jnp.where(before < after, 1.0, 0.0).astype(bf16)
+    owner_row = lax.broadcasted_iota(jnp.int32, (owner_count, LANES), 0)
+
+    def rank_slots(h):
         part = slice(h * ROWS, (h + 1) * ROWS)
-        lead, onehot = leads[h], onehots[h]
         slot = (
-            (2 * step + h) * chunk
+            (CHUNKS * step + h) * chunk
             + lax.broadcasted_iota(jnp.int32, (ROWS, LANES), 0) * LANES
             + lax.broadcasted_iota(jnp.int32, (ROWS, LANES), 1)
         )
         alive = slot < live_ref[0, 0]
         dest = jnp.where(alive, owner_ref[part], owner_count)
         destf = dest.astype(f32)
-
-        for j in range(ROWS):
-            t, half = j // 2, j % 2
-            spread(
-                owners.at[t * owner_count : (t + 1) * owner_count],
-                destf[j : j + 1, :], slice(half * LANES, (half + 1) * LANES), owner_count,
-            )
-        before = lax.broadcasted_iota(jnp.int32, (COLUMNS, COLUMNS + LANES), 0)
-        after = lax.broadcasted_iota(jnp.int32, (COLUMNS, COLUMNS + LANES), 1)
-        upper = jnp.where(before < after, 1.0, 0.0).astype(bf16)
-        prior = lax.dot_general(owners[...], upper, NN, preferred_element_type=f32)
-        owner_row = lax.broadcasted_iota(jnp.int32, (owner_count, LANES), 0)
         start = base[...]
         running = start * float(chunk)
+        owners = jnp.concatenate(
+            [spread(pair(destf, t), owner_count) for t in range(ROWS // 2)], axis=0
+        )
+        priors = lax.dot_general(owners, upper, NN, preferred_element_type=f32)
         for t in range(ROWS // 2):
-            rows = slice(t * owner_count, (t + 1) * owner_count)
+            prior = priors[t * owner_count : (t + 1) * owner_count]
             for half in range(2):
                 j = 2 * t + half
-                total = prior[rows, half * LANES : (half + 1) * LANES] + running
+                total = prior[:, half * LANES : (half + 1) * LANES] + running
                 combined[j : j + 1, :] = jnp.sum(
                     jnp.where(dest[j : j + 1, :] == owner_row, total, 0.0), axis=0, keepdims=True
                 )
-            running = running + prior[rows, COLUMNS:]
+            running = running + prior[:, COLUMNS:]
         tally = running - start * float(chunk)
         base[...] = start + tally
-        pending[h] = start
         both = combined[...].astype(jnp.int32)
         local_rank = both & (chunk - 1)
         rank = local_rank + (both >> 11)
         column = (dest // groups) * RES + (rank & (RES - 1))
         turn = jnp.where(alive, local_rank >> 6, -1)
-
         fields = [
             vel_ref[0, part], vel_ref[1, part], vel_ref[2, part], rate_ref[part], mass_ref[part],
             off_ref[part], cell_ref[part].astype(f32),
         ]
         for v, field in enumerate(fields):
             hi, lo = split2(field)
-            values[v] = hi
-            values[v + FIELDS] = lo
+            values[h, v] = hi
+            values[h, v + FIELDS] = lo
         group = (dest & (groups - 1)).astype(f32)
-        numbers = short_iota(groups)
-        for j in range(ROWS):
-            same = short_rows(group[j : j + 1, :])
-            masks = [same == numbers[b * 16 : (b + 1) * 16] for b in range(groups // 16)]
-            for v in range(2 * FIELDS):
-                value = short_rows(values[v, j : j + 1, :])
-                for b, mask in enumerate(masks):
-                    at = v * groups + b * 16
-                    lead[at : at + 16, j * LANES : (j + 1) * LANES] = jnp.where(mask, value, zero)
-        write_onehot(onehot, jnp.where(turn == 0, column, -1).astype(f32))
         passes = (jnp.max(tally).astype(jnp.int32) + RES - 1) >> 6
-        return passes, turn, column, start
-
-    def further(h, state):
-        passes, turn, column, start = state
-
-        @pl.when(passes > 1)
+        return passes, turn, column, group, start
+
+    def one_pass(h, state, number):
+        _, turn, column, group, start = state
+        picked = jnp.where(turn == number, column, -1).astype(f32)
+        add_product(multiply(group, picked, h), start, number)
+
+    states = [rank_slots(h) for h in range(CHUNKS)]
+    for h in range(CHUNKS):
+        one_pass(h, states[h], 0)
+    for h in range(CHUNKS):
+        @pl.when(states[h][0] > 1)
         def _():
-            def one_pass(number, carry):
-                write_onehot(spare, jnp.where(turn == number, column, -1).astype(f32))
-                add_product(leads[h], spare, start, number)
+            def body(number, carry):
+                one_pass(h, states[h], number)
                 return carry
 
-            lax.fori_loop(1, passes, one_pass, 0)
-
-    late = pending[1]
-    states = [build(0)]
-    add_product(lead1, onehot1, late, 0)
-    states.append(build(1))
-    add_product(lead0, onehot0, pending[0], 0)
-    for h in range(2):
-        further(h, states[h])
+            lax.fori_loop(1, states[h][0], body, 0)
 
     @pl.when(step == pl.num_programs(0) - 1)
     def _():
-        add_product(lead1, onehot1, pending[1], 0)
         low = lax.broadcasted_iota(jnp.int32, (8, LANES), 1) < RES
         for v in range(FIELDS):
             for k in range(COLUMNS // LANES):
@@ -192,28 +191,22 @@
 def dispatch(live, vel, rate, mass, off, owner, cell, owner_count, capacity):
     rows = rate.shape[0]
     groups = owner_count * RES // COLUMNS
-    chunk = ROWS * LANES
     pitch = FIELDS * capacity // LANES
-    plain = pl.BlockSpec((2 * ROWS, LANES), lambda i: (i, 0))
-    lead = pltpu.VMEM((2 * FIELDS * groups, chunk), jnp.bfloat16)
-    onehot = pltpu.VMEM((COLUMNS, chunk), jnp.bfloat16)
+    plain = pl.BlockSpec((CHUNKS * ROWS, LANES), lambda i: (i, 0))
     return pl.pallas_call(
         dispatch_kernel,
-        grid=(rows // (2 * ROWS),),
+        grid=(rows // (CHUNKS * ROWS),),
         in_specs=[
             pl.BlockSpec(memory_space=pltpu.SMEM),
-            pl.BlockSpec((3, 2 * ROWS, LANES), lambda i: (0, i, 0)),
+            pl.BlockSpec((3, CHUNKS * ROWS, LANES), lambda i: (0, i, 0)),
             plain, plain, plain, plain, plain,
         ],
         out_specs=pl.BlockSpec((owner_count * pitch, LANES), lambda i: (0, 0)),
         out_shape=jax.ShapeDtypeStruct((owner_count * pitch, LANES), jnp.float32),
         scratch_shapes=[
             pltpu.VMEM((FIELDS, capacity // RES, groups, COLUMNS), jnp.float32),
-            pltpu.VMEM((2 * FIELDS, ROWS, LANES), jnp.float32),
-            lead, lead, onehot, onehot, onehot,
-            pltpu.VMEM((ROWS // 2 * owner_count, COLUMNS), jnp.bfloat16),
+            pltpu.VMEM((CHUNKS, 2 * FIELDS, ROWS, LANES), jnp.float32),
             pltpu.VMEM((owner_count, LANES), jnp.float32),
-            pltpu.VMEM((2, owner_count, LANES), jnp.float32),
             pltpu.VMEM((ROWS, LANES), jnp.float32),
         ],
         compiler_params=pltpu.CompilerParams(vmem_limit_bytes=60 * 1024 * 1024),
@@ -224,7 +217,7 @@
 def deposit_kernel(
     arrived_ref, gas_ref, sound_ref,
     moved_ref, raw_ref, to_right_ref, to_left_ref, to_other_ref,
-    table, total, onehot0, onehot1, lead0, lead1, speeds, pieces,
+    table, total, speeds, pieces,
 ):
     capacity = moved_ref.shape[2]
     width_x = gas_ref.shape[1]
@@ -232,12 +225,11 @@
     strips = 8
     rows = width_x * strips
     half = 3 * reach * strips
-    pitch = arrived_ref.shape[0] // (2 * SOURCES)
+    pitch = arrived_ref.shape[0] // (BLOCKS * SOURCES)
     parts = capacity // LANES
+    units = [(s, m) for m in range(parts) for s in range(SOURCES)]
     f32, bf16 = jnp.float32, jnp.bfloat16
     step = pl.program_id(0)
-    leads = (lead0, lead1)
-    onehots = (onehot0, onehot1)
 
     @pl.when(step == 0)
     def _():
@@ -252,18 +244,26 @@
                     table[at : at + 16, cols] = hi.astype(bf16)
                     table[3 * rows + at : 3 * rows + at + 16, cols] = lo.astype(bf16)
 
-    one = jnp.ones((16, capacity), bf16)
-    zero = jnp.zeros((16, capacity), bf16)
-    number = lax.broadcasted_iota(jnp.int32, (16, capacity), 0)
+    one = jnp.ones((16, COLUMNS), bf16)
+    zero = jnp.zeros((16, COLUMNS), bf16)
+    number = lax.broadcasted_iota(jnp.int32, (16, COLUMNS), 0)
     numbers = [(number + 16 * b).astype(f32).astype(bf16) for b in range(COLUMNS // 16)]
     strip_number = (number & (strips - 1)).astype(f32).astype(bf16)
-    row_row = lax.broadcasted_iota(jnp.int32, (rows, capacity), 0)
+    row_row = lax.broadcasted_iota(jnp.int32, (rows, LANES), 0)
+
+    def cut(x, unit):
+        s, m = unit
+        return x[s : s + 1, m * LANES : (m + 1) * LANES]
+
+    def pair(x, u):
+        return jnp.concatenate([cut(x, units[u]), cut(x, units[u + 1])], axis=1)
 
     def short_rows(row):
-        return jnp.broadcast_to(row, (16, capacity)).astype(bf16)
-
-    def spans(s):
-        return slice(s * capacity, (s + 1) * capacity)
+        return jnp.broadcast_to(row, (16, COLUMNS)).astype(bf16)
+
+    def spread(column, u):
+        same = short_rows(pair(column, u))
+        return jnp.concatenate([jnp.where(same == n, one, zero) for n in numbers], axis=0)
 
     def field(h, v):
         first = h * SOURCES * pitch + v * parts
@@ -274,27 +274,26 @@
     def look_up(h):
         cell = field(h, 6).astype(jnp.int32)
         column = ((cell & (LANES - 1)) + ((cell >> 10) & 1) * LANES).astype(f32)
-        for s in range(SOURCES):
-            same = short_rows(column[s : s + 1, :])
-            for b in range(COLUMNS // 16):
-                onehots[h][b * 16 : (b + 1) * 16, spans(s)] = jnp.where(
-                    same == numbers[b], one, zero
-                )
-        found = lax.dot_general(table[...], onehots[h][...], NN, preferred_element_type=f32)
-        return cell, found[: 3 * rows] + found[3 * rows :]
-
-    def relax(h, cell, found):
+        strip = (cell >> 7) & (strips - 1)
+        row = (cell >> 11) * strips + strip
+        for u in range(0, len(units), 2):
+            found = lax.dot_general(
+                table[...], spread(column, u), NN, preferred_element_type=f32
+            )
+            found = found[: 3 * rows] + found[3 * rows :]
+            for i in range(2):
+                s, m = units[u + i]
+                mask = cut(row, units[u + i]) == row_row
+                for v in range(3):
+                    mine = found[v * rows : (v + 1) * rows, i * LANES : (i + 1) * LANES]
+                    speeds[h, v, s : s + 1, m * LANES : (m + 1) * LANES] = jnp.sum(
+                        jnp.where(mask, mine, 0.0), axis=0, keepdims=True
+                    )
+        return cell, column, strip.astype(f32)
+
+    def relax(h, cell):
         part = slice(h * SOURCES, (h + 1) * SOURCES)
         plane = cell >> 11
-        strip = (cell >> 7) & (strips - 1)
-        row = plane * strips + strip
-        for s in range(SOURCES):
-            mask = row[s : s + 1, :] == row_row
-            for v in range(3):
-                speeds[v, s : s + 1, :] = jnp.sum(
-                    jnp.where(mask, found[v * rows : (v + 1) * rows, spans(s)], 0.0),
-                    axis=0, keepdims=True,
-                )
         rate = field(h, 3)
         mass = field(h, 4)
         shift = field(h, 5)
@@ -309,43 +308,39 @@
             weights.append(jnp.where(plane == x, low_weight, rest))
         for v in range(3):
             speed = field(h, v)
-            slip = speed - speeds[v]
+            slip = speed - speeds[h, v]
             moved_ref[v, part] = jnp.where(occupied, speed - rate * slip, 0.0)
             kick = mass * rate * slip
             for x in range(reach):
                 hi, lo = split2(kick * weights[x])
-                pieces[v * reach + x] = hi
-                pieces[(3 + v) * reach + x] = lo
-        stripf = strip.astype(f32)
-        for s in range(SOURCES):
-            mask = short_rows(stripf[s : s + 1, :]) == strip_number
-            for pair in range(3 * reach):
+                pieces[h, v * reach + x] = hi
+                pieces[h, (3 + v) * reach + x] = lo
+
+    def gather_up(h, column, strip):
+        product = None
+        for u in range(0, len(units), 2):
+            mask = short_rows(pair(strip, u)) == strip_number
+            blocks = []
+            for p in range(3 * reach):
                 both = [
-                    jnp.broadcast_to(pieces[2 * pair + i, s : s + 1, :], (strips, capacity))
+                    jnp.broadcast_to(pair(pieces[h, 2 * p + i], u), (strips, COLUMNS))
                     for i in range(2)
                 ]
-                leads[h][pair * 16 : (pair + 1) * 16, spans(s)] = jnp.where(
-                    mask, jnp.concatenate(both, axis=0).astype(bf16), zero
-                )
-
-    def gather_up(h, keep):
-        product = lax.dot_general(leads[h][...], onehots[h][...], NT, preferred_element_type=f32)
-        product = product[:half] + product[half:]
-        if keep is not None:
-            product = jnp.where(keep, product, 0.0)
-        total[...] = total[...] + product
-
-    found = look_up(0)
-    gather_up(1, step > 0)
-    relax(0, *found)
-    found = look_up(1)
-    gather_up(0, None)
-    relax(1, *found)
+                blocks.append(jnp.where(mask, jnp.concatenate(both, axis=0).astype(bf16), zero))
+            part = lax.dot_general(
+                jnp.concatenate(blocks, axis=0), spread(column, u), NT, preferred_element_type=f32
+            )
+            product = part if product is None else product + part
+        total[...] = total[...] + (product[:half] + product[half:])
+
+    found = [look_up(h) for h in range(BLOCKS)]
+    for h in range(BLOCKS):
+        relax(h, found[h][0])
+    for h in range(BLOCKS):
+        gather_up(h, *found[h][1:])
 
     @pl.when(step == pl.num_programs(0) - 1)
     def _():
-        gather_up(1, None)
-
         def added(v, x):
             at = (v * reach + x) * strips
             return jnp.concatenate(
@@ -382,17 +377,15 @@
     def whole(shape):
         return pl.BlockSpec(shape, lambda i: (0,) * len(shape))
 
-    onehot = pltpu.VMEM((COLUMNS, SOURCES * capacity), jnp.bfloat16)
-    lead = pltpu.VMEM((2 * deposit_rows, SOURCES * capacity), jnp.bfloat16)
     return pl.pallas_call(
         deposit_kernel,
-        grid=(count // (2 * SOURCES),),
+        grid=(count // (BLOCKS * SOURCES),),
         in_specs=[
-            pl.BlockSpec((2 * SOURCES * pitch, LANES), lambda i: (i, 0)),
+            pl.BlockSpec((BLOCKS * SOURCES * pitch, LANES), lambda i: (i, 0)),
             whole(gas.shape),
             whole(sound.shape),
         ],
-        out_specs=[pl.BlockSpec((3, 2 * SOURCES, capacity), lambda i: (0, i, 0))]
+        out_specs=[pl.BlockSpec((3, BLOCKS * SOURCES, capacity), lambda i: (0, i, 0))]
         + [whole(shape) for shape in shapes],
         out_shape=[
             jax.ShapeDtypeStruct(shape, jnp.float32) for shape in [(3, count, capacity)] + shapes
@@ -400,9 +393,8 @@
         scratch_shapes=[
             pltpu.VMEM((6 * width_x * 8, COLUMNS), jnp.bfloat16),
             pltpu.VMEM((deposit_rows, COLUMNS), jnp.float32),
-            onehot, onehot, lead, lead,
-            pltpu.VMEM((3, SOURCES, capacity), jnp.float32),
-            pltpu.VMEM((6 * reach, SOURCES, capacity), jnp.float32),
+            pltpu.VMEM((BLOCKS, 3, SOURCES, capacity), jnp.float32),
+            pltpu.VMEM((BLOCKS, 6 * reach, SOURCES, capacity), jnp.float32),
         ],
         compiler_params=pltpu.CompilerParams(vmem_limit_bytes=VMEM_BYTES),
         name="deposit",

time: 93.9 us -> 80.5 us (0.86)
  Pallas kernels: 46.1 us -> 32.7 us
    pallas_call x2, Pallas kernels: 45.3 us -> 31.8 us  [the longest x1 17.4 us: dispatch(): pl.pallas_call(dispatch_kernel, grid=(rows // (CHUNKS * ROWS),), in_specs...]
where the time goes in v3:
time: 80.5 us; the launch traced here: 80.2 us
  blocking collectives  33.8 us (42%)
  Pallas kernels  32.7 us (41%)
  waiting for transfers between devices  10.4 us (13%)
  starting transfers between devices  2.1 us (3%)
  between operations  1.29 us (2%)
    all_to_all x1, blocking collectives, per_device(): lax.all_to_all(outbox.reshape(owner_count, 1, FIELDS * capacity), ('tile'...  33.8 us
    pallas_call x1, Pallas kernels, dispatch(): pl.pallas_call(dispatch_kernel, grid=(rows // (CHUNKS * ROWS),), in_specs...  17.4 us
    pallas_call x1, Pallas kernels, deposit(): pl.pallas_call(deposit_kernel, grid=(count // (BLOCKS * SOURCES),), in_sp...  14.4 us
    ppermute x1, waiting for transfers between devices, per_device(): lax.ppermute(jnp.concatenate([mine_right, other[2 * width_x + 1:]]), 'til...  6.85 us
    ppermute x1, waiting for transfers between devices, per_device(): lax.ppermute(jnp.concatenate([mine_left, other[2 * width_x:2 * width_x +...  2.23 us
  transfers between devices with their start and end apart: 3, of which 3 were waited for; matrix products, arithmetic and copies ran while one was open for 0% of the time, Pallas kernels for 0%

profile of v3, /device:TPU:0, one launch (start us, length us, event | category | flops | bytes accessed | tf_op | source)
XLA Modules:
  0.0 80.2 jit_solution(10676850396979024797)
XLA Ops:
  1.3 17.4 %dispatch.1 = f32[2688,128]{1,0:T(8,128)} custom-call(s32[1,1]{1,0:T(1,128)S(6)} %copy.14.live_ref, f32[3,256,128]{2,1,0:T(8,128)} %bitcast.14, f32[256,128]{1,0:T(8,128)} %bitcast.15, f32[256,128]{1,0:T(8,128)} %bitcast.16, f32[256,128]{1,0:T(8,128)} %bitcast.17, s32[256,128]{1,0:T(8,128)} %bitcast.18, s32[256,128]{1,0:T(8,128)} %bitcast.19), custom_call_target="tpu_custom_call" | custom-call | tf_op jit(solution)/shard_map/dispatch/pallas_call | solution.py:196
  18.6 0.0 copy-start
  18.6 0.0 copy-start.1
  18.6 33.8 %all_to_all.5 = f32[128,1,2688]{2,1,0:T(1,128)S(1)} all-to-all(f32[128,1,2688]{2,1,0:T(1,128)} %bitcast.13), channel_id=1, replica_groups=mesh['tile'=64,'slab'=2] {'tile','slab'}, dimensions={0} | all-to-all | bytes 2752512 | tf_op jit(solution)/shard_map/all_to_all | solution.py:505
  52.4 0.0 copy-done
  52.4 0.0 copy-done.1
  52.5 14.4 %deposit.1 = (f32[3,128,384]{2,1,0:T(8,128)}, f32[3,4,16,128]{3,2,1,0:T(8,128)S(1)}, f32[7,16,128]{2,1,0:T(8,128)S(1)}, f32[7,16,128]{2,1,0:T(8,128)S(1)}, f32[10,16,128]{2,1,0:T(8,128)S(1)}) custom-call(f32[2688,128]{1,0:T(8,128)S(1)} %bitcast.12, f32[4,4,16,128]{3,2,1,0:T(8,128)S(1)} %copy-done, f32[4,16,128]{2,1,0:T(8,128)S(1)} %copy-done.1), custom_call_target="tpu_custom_call" | custom-call | tf_op jit(solution)/shard_map/deposit/pallas_call | solution.py:380
  66.9 0.0 collective-permute-start
  66.9 1.3 %collective-permute-done.other_ref = f32[10,16,128]{2,1,0:T(8,128)S(1)} collective-permute-done((f32[10,16,128]{2,1,0:T(8,128)S(1)}, f32[10,16,128]{2,1,0:T(8,128)S(1)}, u32[]{:S(2)}, u32[]{:S(2)}) %collective-permute-start) | collective-permute-done | bytes 81952 | tf_op jit(solution)/shard_map/ppermute | solution.py:512
  68.2 1.5 %collective-permute-start.2 = (f32[8,16,128]{2,1,0:T(8,128)S(1)}, f32[8,16,128]{2,1,0:T(8,128)S(1)}, u32[]{:S(2)}, u32[]{:S(2)}) collective-permute-start(f32[8,16,128]{2,1,0:T(8,128)S(1)} %pad_maximum_fusion.1), channel_id=1, source_target_pairs={{0,126},{2,0},{4,2},{6,4},{8,6},{10,8},{12,10},{14,12},{16,14},{18... | collective-permute-start | bytes 196616 | tf_op jit(solution)/shard_map/ppermute | solution.py:516
  69.7 0.6 collective-permute-start.1
  70.3 2.2 %collective-permute-done.2.right_ref = f32[8,16,128]{2,1,0:T(8,128)S(1)} collective-permute-done((f32[8,16,128]{2,1,0:T(8,128)S(1)}, f32[8,16,128]{2,1,0:T(8,128)S(1)}, u32[]{:S(2)}, u32[]{:S(2)}) %collective-permute-start.2) | collective-permute-done | bytes 65568 | tf_op jit(solution)/shard_map/ppermute | solution.py:516
  72.5 6.9 %collective-permute-done.1.left_ref = f32[8,16,128]{2,1,0:T(8,128)S(1)} collective-permute-done((f32[8,16,128]{2,1,0:T(8,128)S(1)}, f32[8,16,128]{2,1,0:T(8,128)S(1)}, u32[]{:S(2)}, u32[]{:S(2)}) %collective-permute-start.1) | collective-permute-done | bytes 65568 | tf_op jit(solution)/shard_map/ppermute | solution.py:513
  79.4 0.9 %gas_step.1 = f32[4,4,16,128]{3,2,1,0:T(8,128)} custom-call(s32[1,1]{1,0:T(1,128)} %bitcast.slab_ref, f32[4,4,16,128]{3,2,1,0:T(8,128)S(1)} %copy-done, f32[4,16,128]{2,1,0:T(8,128)S(1)} %copy-done.1, f32[3,4,16,128]{3,2,1,0:T(8,128)S(1)} %get-tuple-element.7.raw_ref, f32[7,16,128]{2,1,0:T(8,128)S(1)} %get-tuple-element.8.mine_left_ref, ...), custom_call_target="tpu_custom_call" | custom-call | tf_op jit(solution)/shard_map/gas_step/pallas_call | solution.py:469
  (3 shorter events, 0.0 us)
Async XLA Ops:
  18.6 33.8 %copy-start = (f32[4,4,16,128]{3,2,1,0:T(8,128)S(1)}, f32[4,4,16,128]{3,2,1,0:T(8,128)}, u32[]{:S(2)}) copy-start(f32[4,4,16,128]{3,2,1,0:T(8,128)} %gas_ref.3) | copy-start | bytes 393220
  18.6 33.8 %copy-start.1 = (f32[4,16,128]{2,1,0:T(8,128)S(1)}, f32[4,16,128]{2,1,0:T(8,128)}, u32[]{:S(2)}) copy-start(f32[4,16,128]{2,1,0:T(8,128)} %sound_ref.3) | copy-start | bytes 98308
  66.9 1.3 %collective-permute-start = (f32[10,16,128]{2,1,0:T(8,128)S(1)}, f32[10,16,128]{2,1,0:T(8,128)S(1)}, u32[]{:S(2)}, u32[]{:S(2)}) collective-permute-start(f32[10,16,128]{2,1,0:T(8,128)S(1)} %get-tuple-element.10), channel_id=1, source_target_pairs={{0,1},{1,0},{2,3},{3,2},{4,5},{5,4},{6,7},{7,6},{8,9},{9,8},{10,11... | collective-permute-start | bytes 245768 | tf_op jit(solution)/shard_map/ppermute | solution.py:512
  68.2 4.3 %collective-permute-start.2 = (f32[8,16,128]{2,1,0:T(8,128)S(1)}, f32[8,16,128]{2,1,0:T(8,128)S(1)}, u32[]{:S(2)}, u32[]{:S(2)}) collective-permute-start(f32[8,16,128]{2,1,0:T(8,128)S(1)} %pad_maximum_fusion.1), channel_id=1, source_target_pairs={{0,126},{2,0},{4,2},{6,4},{8,6},{10,8},{12,10},{14,12},{16,14},{18... | collective-permute-start | bytes 196616 | tf_op jit(solution)/shard_map/ppermute | solution.py:516
  69.7 9.7 %collective-permute-start.1 = (f32[8,16,128]{2,1,0:T(8,128)S(1)}, f32[8,16,128]{2,1,0:T(8,128)S(1)}, u32[]{:S(2)}, u32[]{:S(2)}) collective-permute-start(f32[8,16,128]{2,1,0:T(8,128)S(1)} %pad_maximum_fusion), channel_id=1, source_target_pairs={{0,2},{2,4},{4,6},{6,8},{8,10},{10,12},{12,14},{14,16},{16,18},{18... | collective-permute-start | bytes 196616 | tf_op jit(solution)/shard_map/ppermute | solution.py:513

commit v4 on v3

--- a/solution.py
+++ b/solution.py
@@ -11,10 +11,11 @@
 RES = 64
 CHUNKS = 4
 ROWS = 16
-BLOCKS = 4
+BLOCKS = 8
 SOURCES = 8
 FIELDS = 7
 VMEM_BYTES = 40 * 1024 * 1024
+COUNTED = jnp.float8_e4m3fn
 NT = (((1,), (1,)), ((), ()))
 NN = (((1,), (0,)), ((), ()))
 
@@ -100,9 +101,9 @@
                         here, product[v * groups : (v + 1) * groups, cols], 0.0
                     )
 
-    before = lax.broadcasted_iota(jnp.int32, (COLUMNS, COLUMNS + LANES), 0)
-    after = lax.broadcasted_iota(jnp.int32, (COLUMNS, COLUMNS + LANES), 1)
-    upper = jnp.where(before < after, 1.0, 0.0).astype(bf16)
+    before = lax.broadcasted_iota(jnp.int32, (COLUMNS, COLUMNS), 0)
+    after = lax.broadcasted_iota(jnp.int32, (COLUMNS, COLUMNS), 1)
+    upper = jnp.where(before <= after, 1.0, 0.0).astype(COUNTED)
     owner_row = lax.broadcasted_iota(jnp.int32, (owner_count, LANES), 0)
 
     def rank_slots(h):
@@ -120,7 +121,7 @@
         owners = jnp.concatenate(
             [spread(pair(destf, t), owner_count) for t in range(ROWS // 2)], axis=0
         )
-        priors = lax.dot_general(owners, upper, NN, preferred_element_type=f32)
+        priors = lax.dot_general(owners.astype(COUNTED), upper, NN, preferred_element_type=f32)
         for t in range(ROWS // 2):
             prior = priors[t * owner_count : (t + 1) * owner_count]
             for half in range(2):
@@ -129,10 +130,10 @@
                 combined[j : j + 1, :] = jnp.sum(
                     jnp.where(dest[j : j + 1, :] == owner_row, total, 0.0), axis=0, keepdims=True
                 )
-            running = running + prior[:, COLUMNS:]
+            running = running + jnp.broadcast_to(prior[:, COLUMNS - 1 :], (owner_count, LANES))
         tally = running - start * float(chunk)
         base[...] = start + tally
-        both = combined[...].astype(jnp.int32)
+        both = combined[...].astype(jnp.int32) - 1
         local_rank = both & (chunk - 1)
         rank = local_rank + (both >> 11)
         column = (dest // groups) * RES + (rank & (RES - 1))

time: 80.5 us -> 79 us (0.981)
  Pallas kernels: 32.7 us -> 31.3 us
    pallas_call x1, Pallas kernels: 17.4 us -> 16.4 us  [dispatch(): pl.pallas_call(dispatch_kernel, grid=(rows // (CHUNKS * ROWS),), in_specs...]
where the time goes in v4:
time: 79 us; the launch traced here: 78.8 us
  blocking collectives  33.8 us (43%)
  Pallas kernels  31.3 us (40%)
  waiting for transfers between devices  10.4 us (13%)
  starting transfers between devices  2.1 us (3%)
  between operations  1.29 us (2%)
    all_to_all x1, blocking collectives, per_device(): lax.all_to_all(outbox.reshape(owner_count, 1, FIELDS * capacity), ('tile'...  33.8 us
    pallas_call x1, Pallas kernels, dispatch(): pl.pallas_call(dispatch_kernel, grid=(rows // (CHUNKS * ROWS),), in_specs...  16.4 us
    pallas_call x1, Pallas kernels, deposit(): pl.pallas_call(deposit_kernel, grid=(count // (BLOCKS * SOURCES),), in_sp...  14 us
    ppermute x1, waiting for transfers between devices, per_device(): lax.ppermute(jnp.concatenate([mine_right, other[2 * width_x + 1:]]), 'til...  6.85 us
    ppermute x1, waiting for transfers between devices, per_device(): lax.ppermute(jnp.concatenate([mine_left, other[2 * width_x:2 * width_x +...  2.23 us
  transfers between devices with their start and end apart: 3, of which 3 were waited for; matrix products, arithmetic and copies ran while one was open for 0% of the time, Pallas kernels for 0%

profile of v4, /device:TPU:0, one launch (start us, length us, event | category | flops | bytes accessed | tf_op | source)
XLA Modules:
  0.0 78.8 jit_solution(14986336157723568118)
XLA Ops:
  1.3 16.4 %dispatch.1 = f32[2688,128]{1,0:T(8,128)} custom-call(s32[1,1]{1,0:T(1,128)S(6)} %copy.14.live_ref, f32[3,256,128]{2,1,0:T(8,128)} %bitcast.14, f32[256,128]{1,0:T(8,128)} %bitcast.15, f32[256,128]{1,0:T(8,128)} %bitcast.16, f32[256,128]{1,0:T(8,128)} %bitcast.17, s32[256,128]{1,0:T(8,128)} %bitcast.18, s32[256,128]{1,0:T(8,128)} %bitcast.19), custom_call_target="tpu_custom_call" | custom-call | tf_op jit(solution)/shard_map/dispatch/pallas_call | solution.py:197
  17.7 0.0 copy-start
  17.7 0.0 copy-start.1
  17.7 33.8 %all_to_all.5 = f32[128,1,2688]{2,1,0:T(1,128)S(1)} all-to-all(f32[128,1,2688]{2,1,0:T(1,128)} %bitcast.13), channel_id=1, replica_groups=mesh['tile'=64,'slab'=2] {'tile','slab'}, dimensions={0} | all-to-all | bytes 2752512 | tf_op jit(solution)/shard_map/all_to_all | solution.py:506
  51.5 0.0 copy-done
  51.5 0.0 copy-done.1
  51.5 14.0 %deposit.1 = (f32[3,128,384]{2,1,0:T(8,128)}, f32[3,4,16,128]{3,2,1,0:T(8,128)S(1)}, f32[7,16,128]{2,1,0:T(8,128)S(1)}, f32[7,16,128]{2,1,0:T(8,128)S(1)}, f32[10,16,128]{2,1,0:T(8,128)S(1)}) custom-call(f32[2688,128]{1,0:T(8,128)S(1)} %bitcast.12, f32[4,4,16,128]{3,2,1,0:T(8,128)S(1)} %copy-done, f32[4,16,128]{2,1,0:T(8,128)S(1)} %copy-done.1), custom_call_target="tpu_custom_call" | custom-call | tf_op jit(solution)/shard_map/deposit/pallas_call | solution.py:381
  65.5 0.0 collective-permute-start
  65.5 1.3 %collective-permute-done.other_ref = f32[10,16,128]{2,1,0:T(8,128)S(1)} collective-permute-done((f32[10,16,128]{2,1,0:T(8,128)S(1)}, f32[10,16,128]{2,1,0:T(8,128)S(1)}, u32[]{:S(2)}, u32[]{:S(2)}) %collective-permute-start) | collective-permute-done | bytes 81952 | tf_op jit(solution)/shard_map/ppermute | solution.py:513
  66.8 1.5 %collective-permute-start.2 = (f32[8,16,128]{2,1,0:T(8,128)S(1)}, f32[8,16,128]{2,1,0:T(8,128)S(1)}, u32[]{:S(2)}, u32[]{:S(2)}) collective-permute-start(f32[8,16,128]{2,1,0:T(8,128)S(1)} %pad_maximum_fusion.1), channel_id=1, source_target_pairs={{0,126},{2,0},{4,2},{6,4},{8,6},{10,8},{12,10},{14,12},{16,14},{18... | collective-permute-start | bytes 196616 | tf_op jit(solution)/shard_map/ppermute | solution.py:517
  68.3 0.6 collective-permute-start.1
  68.9 2.2 %collective-permute-done.2.right_ref = f32[8,16,128]{2,1,0:T(8,128)S(1)} collective-permute-done((f32[8,16,128]{2,1,0:T(8,128)S(1)}, f32[8,16,128]{2,1,0:T(8,128)S(1)}, u32[]{:S(2)}, u32[]{:S(2)}) %collective-permute-start.2) | collective-permute-done | bytes 65568 | tf_op jit(solution)/shard_map/ppermute | solution.py:517
  71.1 6.9 %collective-permute-done.1.left_ref = f32[8,16,128]{2,1,0:T(8,128)S(1)} collective-permute-done((f32[8,16,128]{2,1,0:T(8,128)S(1)}, f32[8,16,128]{2,1,0:T(8,128)S(1)}, u32[]{:S(2)}, u32[]{:S(2)}) %collective-permute-start.1) | collective-permute-done | bytes 65568 | tf_op jit(solution)/shard_map/ppermute | solution.py:514
  78.0 0.9 %gas_step.1 = f32[4,4,16,128]{3,2,1,0:T(8,128)} custom-call(s32[1,1]{1,0:T(1,128)} %bitcast.slab_ref, f32[4,4,16,128]{3,2,1,0:T(8,128)S(1)} %copy-done, f32[4,16,128]{2,1,0:T(8,128)S(1)} %copy-done.1, f32[3,4,16,128]{3,2,1,0:T(8,128)S(1)} %get-tuple-element.7.raw_ref, f32[7,16,128]{2,1,0:T(8,128)S(1)} %get-tuple-element.8.mine_left_ref, ...), custom_call_target="tpu_custom_call" | custom-call | tf_op jit(solution)/shard_map/gas_step/pallas_call | solution.py:470
  (3 shorter events, 0.0 us)
Async XLA Ops:
  17.7 33.8 %copy-start = (f32[4,4,16,128]{3,2,1,0:T(8,128)S(1)}, f32[4,4,16,128]{3,2,1,0:T(8,128)}, u32[]{:S(2)}) copy-start(f32[4,4,16,128]{3,2,1,0:T(8,128)} %gas_ref.3) | copy-start | bytes 393220
  17.7 33.8 %copy-start.1 = (f32[4,16,128]{2,1,0:T(8,128)S(1)}, f32[4,16,128]{2,1,0:T(8,128)}, u32[]{:S(2)}) copy-start(f32[4,16,128]{2,1,0:T(8,128)} %sound_ref.3) | copy-start | bytes 98308
  65.5 1.3 %collective-permute-start = (f32[10,16,128]{2,1,0:T(8,128)S(1)}, f32[10,16,128]{2,1,0:T(8,128)S(1)}, u32[]{:S(2)}, u32[]{:S(2)}) collective-permute-start(f32[10,16,128]{2,1,0:T(8,128)S(1)} %get-tuple-element.10), channel_id=1, source_target_pairs={{0,1},{1,0},{2,3},{3,2},{4,5},{5,4},{6,7},{7,6},{8,9},{9,8},{10,11... | collective-permute-start | bytes 245768 | tf_op jit(solution)/shard_map/ppermute | solution.py:513
  66.8 4.3 %collective-permute-start.2 = (f32[8,16,128]{2,1,0:T(8,128)S(1)}, f32[8,16,128]{2,1,0:T(8,128)S(1)}, u32[]{:S(2)}, u32[]{:S(2)}) collective-permute-start(f32[8,16,128]{2,1,0:T(8,128)S(1)} %pad_maximum_fusion.1), channel_id=1, source_target_pairs={{0,126},{2,0},{4,2},{6,4},{8,6},{10,8},{12,10},{14,12},{16,14},{18... | collective-permute-start | bytes 196616 | tf_op jit(solution)/shard_map/ppermute | solution.py:517
  68.3 9.7 %collective-permute-start.1 = (f32[8,16,128]{2,1,0:T(8,128)S(1)}, f32[8,16,128]{2,1,0:T(8,128)S(1)}, u32[]{:S(2)}, u32[]{:S(2)}) collective-permute-start(f32[8,16,128]{2,1,0:T(8,128)S(1)} %pad_maximum_fusion), channel_id=1, source_target_pairs={{0,2},{2,4},{4,6},{6,8},{8,10},{10,12},{12,14},{14,16},{16,18},{18... | collective-permute-start | bytes 196616 | tf_op jit(solution)/shard_map/ppermute | solution.py:514

commit v5 on v4

--- a/solution.py
+++ b/solution.py
@@ -1,3 +1,5 @@
+import functools
+
 import jax
 import jax.numpy as jnp
 from jax import lax
@@ -147,8 +149,7 @@
             values[h, v] = hi
             values[h, v + FIELDS] = lo
         group = (dest & (groups - 1)).astype(f32)
-        passes = (jnp.max(tally).astype(jnp.int32) + RES - 1) >> 6
-        return passes, turn, column, group, start
+        return tally, turn, column, group, start
 
     def one_pass(h, state, number):
         _, turn, column, group, start = state
@@ -158,14 +159,18 @@
     states = [rank_slots(h) for h in range(CHUNKS)]
     for h in range(CHUNKS):
         one_pass(h, states[h], 0)
-    for h in range(CHUNKS):
-        @pl.when(states[h][0] > 1)
-        def _():
+
+    def passes(tally):
+        return (jnp.max(tally).astype(jnp.int32) + RES - 1) >> 6
+
+    @pl.when(passes(functools.reduce(jnp.maximum, [state[0] for state in states])) > 1)
+    def _():
+        for h in range(CHUNKS):
             def body(number, carry):
                 one_pass(h, states[h], number)
                 return carry
 
-            lax.fori_loop(1, states[h][0], body, 0)
+            lax.fori_loop(1, passes(states[h][0]), body, 0)
 
     @pl.when(step == pl.num_programs(0) - 1)
     def _():

time: 79 us -> 78.9 us (level)
  no operation moved by 1% of the time
where the time goes in v5:
time: 78.9 us; the launch traced here: 78.7 us
  blocking collectives  33.8 us (43%)
  Pallas kernels  31.1 us (39%)
  waiting for transfers between devices  10.4 us (13%)
  starting transfers between devices  2.1 us (3%)
  between operations  1.29 us (2%)
    all_to_all x1, blocking collectives, per_device(): lax.all_to_all(outbox.reshape(owner_count, 1, FIELDS * capacity), ('tile'...  33.8 us
    pallas_call x1, Pallas kernels, dispatch(): pl.pallas_call(dispatch_kernel, grid=(rows // (CHUNKS * ROWS),), in_specs...  16.3 us
    pallas_call x1, Pallas kernels, deposit(): pl.pallas_call(deposit_kernel, grid=(count // (BLOCKS * SOURCES),), in_sp...  14 us
    ppermute x1, waiting for transfers between devices, per_device(): lax.ppermute(jnp.concatenate([mine_right, other[2 * width_x + 1:]]), 'til...  6.87 us
    ppermute x1, waiting for transfers between devices, per_device(): lax.ppermute(jnp.concatenate([mine_left, other[2 * width_x:2 * width_x +...  2.23 us
  transfers between devices with their start and end apart: 3, of which 3 were waited for; matrix products, arithmetic and copies ran while one was open for 0% of the time, Pallas kernels for 0%

profile of v5, /device:TPU:0, one launch (start us, length us, event | category | flops | bytes accessed | tf_op | source)
XLA Modules:
  0.0 78.7 jit_solution(5392151453157565133)
XLA Ops:
  1.3 16.3 %dispatch.1 = f32[2688,128]{1,0:T(8,128)} custom-call(s32[1,1]{1,0:T(1,128)S(6)} %copy.14.live_ref, f32[3,256,128]{2,1,0:T(8,128)} %bitcast.14, f32[256,128]{1,0:T(8,128)} %bitcast.15, f32[256,128]{1,0:T(8,128)} %bitcast.16, f32[256,128]{1,0:T(8,128)} %bitcast.17, s32[256,128]{1,0:T(8,128)} %bitcast.18, s32[256,128]{1,0:T(8,128)} %bitcast.19), custom_call_target="tpu_custom_call" | custom-call | tf_op jit(solution)/shard_map/dispatch/pallas_call | solution.py:202
  17.6 0.0 copy-start
  17.6 0.0 copy-start.1
  17.6 33.8 %all_to_all.5 = f32[128,1,2688]{2,1,0:T(1,128)S(1)} all-to-all(f32[128,1,2688]{2,1,0:T(1,128)} %bitcast.13), channel_id=1, replica_groups=mesh['tile'=64,'slab'=2] {'tile','slab'}, dimensions={0} | all-to-all | bytes 2752512 | tf_op jit(solution)/shard_map/all_to_all | solution.py:511
  51.4 0.0 copy-done
  51.4 0.0 copy-done.1
  51.4 14.0 %deposit.1 = (f32[3,128,384]{2,1,0:T(8,128)}, f32[3,4,16,128]{3,2,1,0:T(8,128)S(1)}, f32[7,16,128]{2,1,0:T(8,128)S(1)}, f32[7,16,128]{2,1,0:T(8,128)S(1)}, f32[10,16,128]{2,1,0:T(8,128)S(1)}) custom-call(f32[2688,128]{1,0:T(8,128)S(1)} %bitcast.12, f32[4,4,16,128]{3,2,1,0:T(8,128)S(1)} %copy-done, f32[4,16,128]{2,1,0:T(8,128)S(1)} %copy-done.1), custom_call_target="tpu_custom_call" | custom-call | tf_op jit(solution)/shard_map/deposit/pallas_call | solution.py:386
  65.4 0.0 collective-permute-start
  65.4 1.3 %collective-permute-done.other_ref = f32[10,16,128]{2,1,0:T(8,128)S(1)} collective-permute-done((f32[10,16,128]{2,1,0:T(8,128)S(1)}, f32[10,16,128]{2,1,0:T(8,128)S(1)}, u32[]{:S(2)}, u32[]{:S(2)}) %collective-permute-start) | collective-permute-done | bytes 81952 | tf_op jit(solution)/shard_map/ppermute | solution.py:518
  66.7 1.5 %collective-permute-start.2 = (f32[8,16,128]{2,1,0:T(8,128)S(1)}, f32[8,16,128]{2,1,0:T(8,128)S(1)}, u32[]{:S(2)}, u32[]{:S(2)}) collective-permute-start(f32[8,16,128]{2,1,0:T(8,128)S(1)} %pad_maximum_fusion.1), channel_id=1, source_target_pairs={{0,126},{2,0},{4,2},{6,4},{8,6},{10,8},{12,10},{14,12},{16,14},{18... | collective-permute-start | bytes 196616 | tf_op jit(solution)/shard_map/ppermute | solution.py:522
  68.2 0.6 collective-permute-start.1
  68.8 2.2 %collective-permute-done.2.right_ref = f32[8,16,128]{2,1,0:T(8,128)S(1)} collective-permute-done((f32[8,16,128]{2,1,0:T(8,128)S(1)}, f32[8,16,128]{2,1,0:T(8,128)S(1)}, u32[]{:S(2)}, u32[]{:S(2)}) %collective-permute-start.2) | collective-permute-done | bytes 65568 | tf_op jit(solution)/shard_map/ppermute | solution.py:522
  71.0 6.9 %collective-permute-done.1.left_ref = f32[8,16,128]{2,1,0:T(8,128)S(1)} collective-permute-done((f32[8,16,128]{2,1,0:T(8,128)S(1)}, f32[8,16,128]{2,1,0:T(8,128)S(1)}, u32[]{:S(2)}, u32[]{:S(2)}) %collective-permute-start.1) | collective-permute-done | bytes 65568 | tf_op jit(solution)/shard_map/ppermute | solution.py:519
  77.9 0.9 %gas_step.1 = f32[4,4,16,128]{3,2,1,0:T(8,128)} custom-call(s32[1,1]{1,0:T(1,128)} %bitcast.slab_ref, f32[4,4,16,128]{3,2,1,0:T(8,128)S(1)} %copy-done, f32[4,16,128]{2,1,0:T(8,128)S(1)} %copy-done.1, f32[3,4,16,128]{3,2,1,0:T(8,128)S(1)} %get-tuple-element.7.raw_ref, f32[7,16,128]{2,1,0:T(8,128)S(1)} %get-tuple-element.8.mine_left_ref, ...), custom_call_target="tpu_custom_call" | custom-call | tf_op jit(solution)/shard_map/gas_step/pallas_call | solution.py:475
  (3 shorter events, 0.0 us)
Async XLA Ops:
  17.6 33.8 %copy-start = (f32[4,4,16,128]{3,2,1,0:T(8,128)S(1)}, f32[4,4,16,128]{3,2,1,0:T(8,128)}, u32[]{:S(2)}) copy-start(f32[4,4,16,128]{3,2,1,0:T(8,128)} %gas_ref.3) | copy-start | bytes 393220
  17.6 33.8 %copy-start.1 = (f32[4,16,128]{2,1,0:T(8,128)S(1)}, f32[4,16,128]{2,1,0:T(8,128)}, u32[]{:S(2)}) copy-start(f32[4,16,128]{2,1,0:T(8,128)} %sound_ref.3) | copy-start | bytes 98308
  65.4 1.3 %collective-permute-start = (f32[10,16,128]{2,1,0:T(8,128)S(1)}, f32[10,16,128]{2,1,0:T(8,128)S(1)}, u32[]{:S(2)}, u32[]{:S(2)}) collective-permute-start(f32[10,16,128]{2,1,0:T(8,128)S(1)} %get-tuple-element.10), channel_id=1, source_target_pairs={{0,1},{1,0},{2,3},{3,2},{4,5},{5,4},{6,7},{7,6},{8,9},{9,8},{10,11... | collective-permute-start | bytes 245768 | tf_op jit(solution)/shard_map/ppermute | solution.py:518
  66.7 4.3 %collective-permute-start.2 = (f32[8,16,128]{2,1,0:T(8,128)S(1)}, f32[8,16,128]{2,1,0:T(8,128)S(1)}, u32[]{:S(2)}, u32[]{:S(2)}) collective-permute-start(f32[8,16,128]{2,1,0:T(8,128)S(1)} %pad_maximum_fusion.1), channel_id=1, source_target_pairs={{0,126},{2,0},{4,2},{6,4},{8,6},{10,8},{12,10},{14,12},{16,14},{18... | collective-permute-start | bytes 196616 | tf_op jit(solution)/shard_map/ppermute | solution.py:522
  68.2 9.7 %collective-permute-start.1 = (f32[8,16,128]{2,1,0:T(8,128)S(1)}, f32[8,16,128]{2,1,0:T(8,128)S(1)}, u32[]{:S(2)}, u32[]{:S(2)}) collective-permute-start(f32[8,16,128]{2,1,0:T(8,128)S(1)} %pad_maximum_fusion), channel_id=1, source_target_pairs={{0,2},{2,4},{4,6},{6,8},{8,10},{10,12},{12,14},{14,16},{16,18},{18... | collective-permute-start | bytes 196616 | tf_op jit(solution)/shard_map/ppermute | solution.py:519
